TPU v7x, 32 devices: a whole 2x2x4 slice. The times are simulated.
32 devices in a mesh: band: 2 (over x), tile: 8 (over z, y), lvl: 2 (over core).
Axes of the slice: x: 2, y: 2, z: 4, core: 2. Of those that a mesh axis runs over, the one named last changes fastest.
Arguments:
- image: float32 [512, 4096], P('band', 'tile'), parts along dimension 0, may hold values from 0 to 1
- curves: float32 [16, 17], P('lvl'), may hold values from -1 to 1
Outputs:
- toned: float32 [512, 4096], P('band', 'tile'), parts along dimension 0
There are 2 independent parts, one for each index of `band`. A program takes and returns all parts, laid end to end along the dimension named above; an argument that names none is the same for every part. Nothing has to cross between parts.
All inputs are finite; a program needn't handle non-finite values.
Results may differ from a plain program's by a relative error of at most 0.0003.
Values sent between devices are 32-bit elements; how exact they have to be, the bound alone decides.
No kernel may reach another device: no remote copies, remote signals or barrier semaphores. Data moves between devices by JAX's collectives and lax.ppermute only.
A program may use at most 64 MiB of HBM per device.

v0:
```python
import functools

import jax
import jax.numpy as jnp
from jax import lax
from jax.experimental import pallas as pl
from jax.experimental.pallas import tpu as pltpu
from jax.sharding import PartitionSpec as P

LEVELS = 16
KNOTS = 17
PYR = 6

SUB = 8
LANES = 128
RIM = 128
COPIES = LEVELS + 1

VMEM = pl.BlockSpec(memory_space=pltpu.VMEM)
HBM = pl.BlockSpec(memory_space=pltpu.HBM)
PARAMS = pltpu.CompilerParams(vmem_limit_bytes=20 * 1024 * 1024)


def iota(shape, dim):
    return lax.broadcasted_iota(jnp.int32, shape, dim)


def down_taps(distance):
    size = jnp.abs(distance)
    value = jnp.where(size == 0, 6.0, jnp.where(size == 1, 4.0, jnp.where(size == 2, 1.0, 0.0)))
    return (value / 256.0).astype(jnp.bfloat16)


def up_taps(distance):
    size = jnp.abs(distance)
    value = jnp.where(size == 0, 0.75, jnp.where(size == 1, 0.5, jnp.where(size == 2, 0.125, 0.0)))
    return (value / 8.0).astype(jnp.bfloat16)


def twice(table):
    return jnp.concatenate([table, table], axis=0)


def halves(x):
    high = x.astype(jnp.bfloat16)
    low = (x - high.astype(jnp.float32)).astype(jnp.bfloat16)
    return jnp.concatenate([high, low], axis=-1)


def dot(x, table):
    return jnp.dot(x, table, preferred_element_type=jnp.float32)


def shift_down(x):
    return pltpu.roll(x, 1, axis=x.ndim - 2)


def shift_up(x):
    return pltpu.roll(x, SUB - 1, axis=x.ndim - 2)


def sublane(x):
    return iota(x.shape, x.ndim - 2)


def rows_down(planes):
    first, last = planes[0], planes[-1]
    top = sublane(first) == 0
    minus2 = jnp.where(top, first, shift_down(planes[-2]))
    minus1 = jnp.where(top, first, shift_down(last))
    plus = jnp.where(sublane(first) == SUB - 1, last, shift_up(first))
    padded = [minus2, minus1] + list(planes) + [plus]
    out = []
    for at in range(0, len(planes), 2):
        a, b, c, d, e = padded[at:at + 5]
        out.append((a + e) + 4.0 * (b + d) + 6.0 * c)
    return out


def padded_for_up(planes):
    first, last = planes[0], planes[-1]
    below = jnp.where(sublane(first) == 0, first, shift_down(last))
    above = jnp.where(sublane(first) == SUB - 1, last, shift_up(first))
    return [below] + list(planes) + [above]


def rows_up(planes):
    padded = padded_for_up(planes)
    out = []
    for at in range(len(planes)):
        a, b, c = padded[at:at + 3]
        out.append((a + c) + 6.0 * b)
        out.append(4.0 * (b + c))
    return out


def look_up(table, index):
    return jnp.take_along_axis(table, index, axis=0, mode="promise_in_bounds")


def cell(x, cells):
    scaled = x * float(cells)
    index = jnp.clip(scaled.astype(jnp.int32), 0, cells - 1)
    return index, scaled - index.astype(jnp.float32)


def curve_tables(curve_row, k):
    steps = (KNOTS - 1) // 2
    turn = steps * k // (LEVELS - 1)
    phase = (steps * k % (LEVELS - 1)) / (LEVELS - 1)
    width = curve_row.shape[-1]
    row = jnp.broadcast_to(curve_row, (SUB, width))
    offset = iota((SUB, width), 1) - iota((SUB, width), 0)

    def node(shift):
        at = jnp.where(offset == steps - turn + shift, row, 0.0)
        return jnp.sum(at, axis=1, keepdims=True)

    left, middle, right = node(-1), node(0), node(1)
    slope = middle - left
    bend = (right - middle) - slope
    start = (k / (LEVELS - 1) + middle) - phase * slope - phase * bend
    spread = lambda v: jnp.broadcast_to(v, (SUB, LANES))
    return spread(start), spread(slope), spread(bend), jnp.full((SUB, LANES), phase, jnp.float32)


def remap(tables, index, rest):
    start, slope, bend, phase = tables
    bent = jnp.maximum(rest, phase)
    return look_up(start, index) + look_up(slope, index) * rest + look_up(bend, index) * bent


def stage_kernel(image_ref, whole_ref, edge_ref, sems):
    lvl = lax.axis_index("lvl")
    tiles = whole_ref.shape[0]
    start = pl.multiple_of(lvl * (tiles - 1) * LANES, LANES)
    copies = [pltpu.make_async_copy(image_ref.at[:, pl.ds(start, RIM)], edge_ref, sems.at[tiles])]
    for tile in range(tiles):
        source = image_ref.at[:, tile * LANES:(tile + 1) * LANES]
        copies.append(pltpu.make_async_copy(source, whole_ref.at[tile], sems.at[tile]))
    for copy in copies:
        copy.start()
    for copy in copies:
        copy.wait()


def put_kernel(half_ref, out_ref, sems, lvl):
    tiles = half_ref.shape[0]
    copies = []
    for tile in range(tiles):
        start = pl.multiple_of((lvl * tiles + tile) * LANES, LANES)
        target = out_ref.at[:, pl.ds(start, LANES)]
        copies.append(pltpu.make_async_copy(half_ref.at[tile], target, sems.at[tile]))
    for copy in copies:
        copy.start()
    for copy in copies:
        copy.wait()


def put_mine_kernel(mine_ref, out_ref, sems):
    put_kernel(mine_ref, out_ref, sems, lax.axis_index("lvl"))


def put_theirs_kernel(theirs_ref, begun_ref, out_ref, sems):
    put_kernel(theirs_ref, out_ref, sems, 1 - lax.axis_index("lvl"))


def pick(index, values):
    low = high = None
    before = None
    for k in range(LEVELS):
        value = values(k)
        mask = index == k if k < LEVELS - 1 else None
        if k == 0:
            low = value
        elif k < LEVELS - 1:
            low = jnp.where(mask, value, low)
        if k == 1:
            high = value
        elif k > 1:
            high = jnp.where(before, value, high)
        before = mask
    return low, high


def own_kernel(image_ref, mine_ref, other_ref, gauss_ref, tone_ref, index_ref, rest_ref, table_ref,
               x_scr, cell_scr, rest_scr, low_scr, high_scr, part_scr, down_scr):
    lvl = lax.axis_index("lvl")
    tiles, rows, _ = image_ref.shape
    planes = rows // SUB
    half = tiles * LANES // 2
    own = half + RIM

    at = iota((own, half), 0)
    place = jnp.where((at >= half) & (lvl == 1), at - own, at)
    down = down_taps(place - 2 * (iota((own, half), 1) - RIM // 2))
    down_scr[0:own, :] = down
    down_scr[own:2 * own, :] = down

    first = jnp.where(lvl == 0, mine_ref[...], other_ref[...])
    second = jnp.where(lvl == 0, other_ref[...], mine_ref[...])
    for k in range(LEVELS):
        source = first if k < LEVELS // 2 else second
        row = k % (LEVELS // 2)
        for kind, table in enumerate(curve_tables(source[row:row + 1, :], k)):
            table_ref[k, kind] = table

    sources = [lvl * (tiles // 2) + tile for tile in range(tiles // 2)] + [tiles // 2 - lvl]
    for p in range(planes):
        for tile, source in enumerate(sources):
            span = slice(tile * LANES, (tile + 1) * LANES)
            x_scr[p, :, span] = image_ref[source, pl.ds(p, SUB, stride=planes), :]
    for p in range(planes):
        x = x_scr[p]
        index, rest = cell(x, (KNOTS - 1) // 2)
        cell_scr[p] = index
        rest_scr[p] = rest
        index, rest = cell(x[:, 0:half], LEVELS - 1)
        index_ref[p] = index
        rest_ref[p] = rest

    def store(k, column, reduced):
        for pair in range(planes // 4):
            both = jnp.concatenate(reduced[2 * pair:2 * pair + 2], axis=0)
            high = both.astype(jnp.bfloat16)
            low = (both - high.astype(jnp.float32)).astype(jnp.bfloat16)
            part_scr[pair, k, :, column:column + LANES] = high
            part_scr[pair, k, :, own + column:own + column + LANES] = low

    def one_copy(k, carry):
        tables = tuple(table_ref[k, kind] for kind in range(4))
        for column in range(0, own, LANES):
            span = slice(column, column + LANES)
            mapped = [remap(tables, cell_scr[p, :, span], rest_scr[p, :, span]) for p in range(planes)]
            if column < half:
                for p in range(planes):
                    index = index_ref[p, :, span]
                    low_scr[p, :, span] = jnp.where(index == k, mapped[p], low_scr[p, :, span])
                    high_scr[p, :, span] = jnp.where(index == k - 1, mapped[p], high_scr[p, :, span])
            store(k, column, rows_down(mapped))
        return carry

    lax.fori_loop(0, LEVELS, one_copy, 0)
    for column in range(0, own, LANES):
        store(LEVELS, column, rows_down([x_scr[p, :, column:column + LANES] for p in range(planes)]))
    for p in range(planes):
        tone_ref[p] = low_scr[p] + rest_ref[p] * (high_scr[p] - low_scr[p])

    part = part_scr[...].reshape(-1, 2 * own)
    gauss_ref[...] = dot(part, down_scr[...]).reshape(gauss_ref.shape)


def rest_kernel(halo_ref, gauss_in_ref, tone_ref, index_ref, rest_ref, table_ref, out_ref,
                x_scr, cell_scr, frac_scr, part_scr, gauss_scr, up_scr):
    lvl = lax.axis_index("lvl")
    rows = halo_ref.shape[0]
    planes = rows // SUB
    half = out_ref.shape[0] * LANES

    for p in range(planes):
        x = halo_ref[pl.ds(p, SUB, stride=planes), :]
        x_scr[p] = x
        index, rest = cell(x, (KNOTS - 1) // 2)
        cell_scr[p] = index
        frac_scr[p] = rest

    def store(k, reduced):
        for pair in range(planes // 4):
            both = jnp.concatenate(reduced[2 * pair:2 * pair + 2], axis=0)
            part_scr[pair, k] = halves(both)

    def one_copy(k, carry):
        tables = tuple(table_ref[k, kind] for kind in range(4))
        store(k, rows_down([remap(tables, cell_scr[p], frac_scr[p]) for p in range(planes)]))
        return carry

    lax.fori_loop(0, LEVELS, one_copy, 0)
    store(LEVELS, rows_down([x_scr[p] for p in range(planes)]))
    at = iota((RIM, LANES), 0)
    place = jnp.where(lvl == 0, at - RIM, at + half)
    target = iota((RIM, LANES), 1) + lvl * LANES - RIM // 2
    share = dot(part_scr[...].reshape(-1, 2 * RIM), twice(down_taps(place - 2 * target)))
    share = share.reshape(planes // 4, COPIES, 2, SUB, LANES)
    near = pl.multiple_of(lvl * LANES, LANES)
    away = pl.multiple_of((1 - lvl) * LANES, LANES)
    gauss_scr[:, :, :, :, pl.ds(near, LANES)] = gauss_in_ref[:, :, :, :, pl.ds(near, LANES)] + share
    gauss_scr[:, :, :, :, pl.ds(away, LANES)] = gauss_in_ref[:, :, :, :, pl.ds(away, LANES)]

    gauss = [None, [gauss_scr[p // 2, :, p % 2] for p in range(planes // 2)]]
    small = down_taps(iota((LANES, LANES), 0) - 2 * iota((LANES, LANES), 1))
    wide = down_taps(iota((half, LANES), 0) - 2 * iota((half, LANES), 1))
    for level in range(1, PYR - 1):
        reduced = rows_down(gauss[level])
        count = len(reduced)
        stacked = jnp.concatenate(reduced, axis=0)
        stacked = stacked.reshape(-1, stacked.shape[-1])
        result = dot(halves(stacked), twice(wide if level == 1 else small))
        result = result.reshape(count, COPIES, SUB, LANES)
        gauss.append([result[p] for p in range(count)])

    full = twice(up_taps(2 * iota((half, half), 0) - (iota((half, half), 1) + RIM)))
    source = gauss_scr[:, 0:LEVELS].reshape(-1, half)
    up_scr[...] = dot(halves(source), full).reshape(up_scr.shape)

    narrow = twice(up_taps(2 * iota((LANES, half), 0) - iota((LANES, half), 1)))
    out = [gauss[PYR - 1][0][LEVELS]]
    for level in range(PYR - 2, 0, -1):
        columns = half if level == 1 else LANES
        table = narrow[:, 0:columns]
        coarse = gauss[level + 1]
        count = len(coarse)
        stacked = jnp.concatenate([plane[0:LEVELS] for plane in coarse], axis=0).reshape(-1, LANES)
        wider = dot(halves(stacked), table).reshape(count, LEVELS, SUB, columns)
        raised = rows_up([wider[p] for p in range(count)])
        base = dot(halves(jnp.concatenate(out, axis=0)), table).reshape(count, SUB, columns)
        base = rows_up([base[p] for p in range(count)])
        out = []
        for p in range(2 * count):
            here = gauss[level][p]
            index, rest = cell(here[LEVELS], LEVELS - 1)
            low, high = pick(index, lambda k: here[k] - raised[p][k])
            out.append(low + rest * (high - low) + base[p])

    base = dot(halves(jnp.concatenate(out, axis=0)), full).reshape(planes // 2, SUB, half)
    base = rows_up([base[p] for p in range(planes // 2)])
    columns_up = [up_scr[p // 2, :, p % 2] for p in range(planes // 2)]
    first, last = columns_up[0], columns_up[-1]
    padded = padded_for_up(columns_up)
    for p in range(planes):
        a, b, c = padded[p // 2], padded[p // 2 + 1], padded[p // 2 + 2]
        if p % 2 == 0:
            low, high = pick(index_ref[p], lambda k: (a[k] + c[k]) + 6.0 * b[k])
            detail = low + rest_ref[p] * (high - low)
        else:
            low, high = pick(index_ref[p], lambda k: b[k] + c[k])
            detail = 4.0 * (low + rest_ref[p] * (high - low))
        toned = (tone_ref[p] - detail) + base[p]
        for tile in range(half // LANES):
            out_ref[tile, pl.ds(p, SUB, stride=planes), :] = toned[:, tile * LANES:(tile + 1) * LANES]


def call(kernel, name, in_specs, out_shape, scratch, out_space=VMEM, **others):
    return pl.pallas_call(
        kernel,
        name=name,
        in_specs=in_specs,
        out_specs=jax.tree.map(lambda _: out_space, out_shape),
        out_shape=out_shape,
        scratch_shapes=scratch,
        compiler_params=PARAMS,
        **others,
    )


def body(image, curves):
    rows, width = image.shape
    half = width // 2
    own = half + RIM
    planes = rows // SUB
    lvl = lax.axis_index("lvl")
    tiles = lax.axis_size("tile")
    f32 = lambda *shape: jax.ShapeDtypeStruct(shape, jnp.float32)
    i32 = lambda *shape: jax.ShapeDtypeStruct(shape, jnp.int32)
    swap = [(0, 1), (1, 0)]

    other_curves = lax.ppermute(curves, "lvl", swap)
    whole, edge = call(
        stage_kernel, "stage", [HBM], [f32(width // LANES, rows, LANES), f32(rows, RIM)],
        [pltpu.SemaphoreType.DMA((width // LANES + 1,))],
    )(image)
    edge, other_curves = lax.optimization_barrier((edge, other_curves))
    pairs = []
    for tile in range(tiles):
        pairs.append((2 * tile + 1, 2 * ((tile + 1) % tiles)))
        pairs.append((2 * tile, 2 * ((tile - 1) % tiles) + 1))
    halo = lax.ppermute(edge, ("tile", "lvl"), pairs)

    gauss, tone, index, rest, tables = call(
        own_kernel, "own", [VMEM] * 3,
        [f32(planes // 4, COPIES, 2, SUB, half), f32(planes, SUB, half), i32(planes, SUB, half),
         f32(planes, SUB, half), f32(LEVELS, 4, SUB, LANES)],
        [pltpu.VMEM((planes, SUB, own), jnp.float32), pltpu.VMEM((planes, SUB, own), jnp.int32),
         pltpu.VMEM((planes, SUB, own), jnp.float32), pltpu.VMEM((planes, SUB, half), jnp.float32),
         pltpu.VMEM((planes, SUB, half), jnp.float32),
         pltpu.VMEM((planes // 4, COPIES, 2 * SUB, 2 * own), jnp.bfloat16),
         pltpu.VMEM((2 * own, half), jnp.bfloat16)],
    )(whole, curves, other_curves)
    mine = call(
        rest_kernel, "rest", [VMEM] * 6, f32(half // LANES, rows, LANES),
        [pltpu.VMEM((planes, SUB, RIM), jnp.float32), pltpu.VMEM((planes, SUB, RIM), jnp.int32),
         pltpu.VMEM((planes, SUB, RIM), jnp.float32),
         pltpu.VMEM((planes // 4, COPIES, 2 * SUB, 2 * RIM), jnp.bfloat16),
         pltpu.VMEM((planes // 4, COPIES, 2, SUB, half), jnp.float32),
         pltpu.VMEM((planes // 4, LEVELS, 2, SUB, half), jnp.float32)],
    )(halo, gauss, tone, index, rest, tables)
    theirs = lax.ppermute(mine, "lvl", swap)
    sems = [pltpu.SemaphoreType.DMA((half // LANES,))]
    begun = call(put_mine_kernel, "put_mine", [VMEM], f32(rows, width), sems, HBM)(mine)
    return call(
        put_theirs_kernel, "put_theirs", [VMEM, HBM], f32(rows, width), sems, HBM, input_output_aliases={1: 0}
    )(theirs, begun)


def solution(mesh):
    placed = (P("band", "tile"), P("lvl", None))
    return jax.shard_map(
        body, mesh=mesh, in_specs=placed, out_specs=P("band", "tile"), check_vma=False
    )
```

profile of v0, /device:TPU:0, one launch (start us, length us, event | category | flops | bytes accessed | tf_op | source)
XLA Modules:
  0.0 22.1 jit_solution(15445355875131325740)
XLA Ops:
  0.0 0.5 %collective-permute-start = (f32[8,17]{1,0:T(8,128)}, f32[8,17]{1,0:T(8,128)S(1)}, u32[]{:S(2)}, u32[]{:S(2)}) collective-permute-start(f32[8,17]{1,0:T(8,128)} %mine_ref.1), channel_id=1, source_target_pairs={{0,1},{1,0},{2,3},{3,2},{4,5},{5,4},{6,7},{7,6},{8,9},{9,8},{10,11... | collective-permute-start | bytes 1640 | tf_op jit(solution)/shard_map/ppermute | solution.py:366
  0.5 0.0 copy-start
  0.5 1.0 %copy-done = f32[256,512]{1,0:T(8,128)S(1)} copy-done((f32[256,512]{1,0:T(8,128)S(1)}, f32[256,512]{1,0:T(8,128)}, u32[]{:S(2)}) %copy-start) | copy-done | bytes 524312
  1.5 0.1 stage.1
  1.6 0.0 collective-permute-done.other_ref
  1.7 5.7 %collective-permute-start.1 = (f32[256,128]{1,0:T(8,128)S(1)}, f32[256,128]{1,0:T(8,128)S(1)}, u32[]{:S(2)}, u32[]{:S(2)}) collective-permute-start(f32[256,128]{1,0:T(8,128)S(1)} %get-tuple-element.15), channel_id=1, source_target_pairs={{1,2},{0,15},{3,4},{2,1},{5,6},{4,3},{7,8},{6,5},{9,10},{8,7},{11,... | collective-permute-start | bytes 393224 | tf_op jit(solution)/shard_map/ppermute | solution.py:376
  7.4 0.0 copy-start.1
  7.4 0.7 %copy-done.1 = f32[8,17]{1,0:T(8,128)S(1)} copy-done((f32[8,17]{1,0:T(8,128)S(1)}, f32[8,17]{1,0:T(8,128)}, u32[]{:S(2)}) %copy-start.1) | copy-done | bytes 568
  8.1 6.0 %own.1 = (f32[8,17,2,8,256]{4,3,2,1,0:T(8,128)S(1)}, f32[32,8,256]{2,1,0:T(8,128)S(1)}, s32[32,8,256]{2,1,0:T(8,128)S(1)}, f32[32,8,256]{2,1,0:T(8,128)S(1)}, f32[16,4,8,128]{3,2,1,0:T(8,128)S(1)}) custom-call(f32[4,256,128]{2,1,0:T(8,128)S(1)} %get-tuple-element.16.image_ref, f32[8,17]{1,0:T(8,128)S(1)} %copy-done.1, f32[8,17]{1,0:T(8,128)S(1)} %collective-permute-done.other_ref), custom_call_target="tpu_custom_call" | custom-call | tf_op jit(solution)/shard_map/own/pallas_call | solution.py:378
  14.1 0.0 collective-permute-done.1.halo_ref
  14.1 5.6 %rest.1.mine_ref = f32[2,256,128]{2,1,0:T(8,128)S(1)} custom-call(f32[256,128]{1,0:T(8,128)S(1)} %collective-permute-done.1.halo_ref, f32[8,17,2,8,256]{4,3,2,1,0:T(8,128)S(1)} %get-tuple-element.18.gauss_in_ref, f32[32,8,256]{2,1,0:T(8,128)S(1)} %get-tuple-element.19.tone_ref, s32[32,8,256]{2,1,0:T(8,128)S(1)} %get-tuple-element.20.index_ref, ...), custom_call_target="tpu_custom_call" | custom-call | tf_op jit(solution)/shard_map/rest/pallas_call | solution.py:388
  19.8 0.1 collective-permute-start.2
  19.9 0.7 %put_mine.1.begun_ref = f32[256,512]{1,0:T(8,128)} custom-call(f32[2,256,128]{2,1,0:T(8,128)S(1)} %rest.1.mine_ref), custom_call_target="tpu_custom_call" | custom-call | tf_op jit(solution)/shard_map/put_mine/pallas_call | solution.py:398
  20.6 0.8 %collective-permute-done.2.theirs_ref = f32[2,256,128]{2,1,0:T(8,128)S(1)} collective-permute-done((f32[2,256,128]{2,1,0:T(8,128)S(1)}, f32[2,256,128]{2,1,0:T(8,128)S(1)}, u32[]{:S(2)}, u32[]{:S(2)}) %collective-permute-start.2) | collective-permute-done | bytes 262176 | tf_op jit(solution)/shard_map/ppermute | solution.py:396
  21.4 0.7 %put_theirs.1 = f32[256,512]{1,0:T(8,128)} custom-call(f32[2,256,128]{2,1,0:T(8,128)S(1)} %collective-permute-done.2.theirs_ref, f32[256,512]{1,0:T(8,128)} %put_mine.1.begun_ref), custom_call_target="tpu_custom_call", output_to_operand_aliasing={{}: (1, {})} | custom-call | tf_op jit(solution)/shard_map/put_theirs/pallas_call | solution.py:399
Async XLA Ops:
  0.0 1.6 %collective-permute-start = (f32[8,17]{1,0:T(8,128)}, f32[8,17]{1,0:T(8,128)S(1)}, u32[]{:S(2)}, u32[]{:S(2)}) collective-permute-start(f32[8,17]{1,0:T(8,128)} %mine_ref.1), channel_id=1, source_target_pairs={{0,1},{1,0},{2,3},{3,2},{4,5},{5,4},{6,7},{7,6},{8,9},{9,8},{10,11... | collective-permute-start | bytes 1640 | tf_op jit(solution)/shard_map/ppermute | solution.py:366
  0.5 1.0 %copy-start = (f32[256,512]{1,0:T(8,128)S(1)}, f32[256,512]{1,0:T(8,128)}, u32[]{:S(2)}) copy-start(f32[256,512]{1,0:T(8,128)} %image_ref.1) | copy-start | bytes 1572868
  1.7 12.5 %collective-permute-start.1 = (f32[256,128]{1,0:T(8,128)S(1)}, f32[256,128]{1,0:T(8,128)S(1)}, u32[]{:S(2)}, u32[]{:S(2)}) collective-permute-start(f32[256,128]{1,0:T(8,128)S(1)} %get-tuple-element.15), channel_id=1, source_target_pairs={{1,2},{0,15},{3,4},{2,1},{5,6},{4,3},{7,8},{6,5},{9,10},{8,7},{11,... | collective-permute-start | bytes 393224 | tf_op jit(solution)/shard_map/ppermute | solution.py:376
  7.4 0.7 %copy-start.1 = (f32[8,17]{1,0:T(8,128)S(1)}, f32[8,17]{1,0:T(8,128)}, u32[]{:S(2)}) copy-start(f32[8,17]{1,0:T(8,128)} %mine_ref.1) | copy-start | bytes 1636
  19.8 1.6 %collective-permute-start.2 = (f32[2,256,128]{2,1,0:T(8,128)S(1)}, f32[2,256,128]{2,1,0:T(8,128)S(1)}, u32[]{:S(2)}, u32[]{:S(2)}) collective-permute-start(f32[2,256,128]{2,1,0:T(8,128)S(1)} %rest.1.mine_ref), channel_id=1, source_target_pairs={{0,1},{1,0},{2,3},{3,2},{4,5},{5,4},{6,7},{7,6},{8,9},{9,8},{10,11... | collective-permute-start | bytes 786440 | tf_op jit(solution)/shard_map/ppermute | solution.py:396
where the time goes:
time: 22.3 us; the launch traced here: 22.1 us
  Pallas kernels  13.3 us (60%)
  starting transfers between devices  6.26 us (28%)
  local copies, waits for them, and re-layouts  1.73 us (8%)
  waiting for transfers between devices  0.8 us (4%)
    pallas_call x1, Pallas kernels, body(): call(own_kernel, 'own', [VMEM] * 3, [f32(planes // 4, COPIES, 2, SUB, hal...  6.04 us
    ppermute x1, starting transfers between devices, body(): halo = lax.ppermute(edge, ('tile', 'lvl'), pairs)  5.73 us
    pallas_call x1, Pallas kernels, body(): call(rest_kernel, 'rest', [VMEM] * 6, f32(half // LANES, rows, LANES), [p...  5.63 us
    unnamed x4, local copies, waits for them, and re-layouts  1.73 us
    ppermute x1, waiting for transfers between devices, body(): theirs = lax.ppermute(mine, 'lvl', swap)  0.79 us
    pallas_call x1, Pallas kernels, body(): call(put_mine_kernel, 'put_mine', [VMEM], f32(rows, width), sems, HBM)(mine)  0.72 us
    pallas_call x1, Pallas kernels, body(): call(put_theirs_kernel, 'put_theirs', [VMEM, HBM], f32(rows, width), sems...  0.71 us
    ppermute x1, starting transfers between devices, body(): other_curves = lax.ppermute(curves, 'lvl', swap)  0.45 us
  transfers between devices with their start and end apart: 3, of which 1 were waited for; matrix products, arithmetic and copies ran while one was open for 0% of the time, Pallas kernels for 31%

commit v1 on v0

v1 whole, which is shorter than its diff:
```python
import functools

import jax
import jax.numpy as jnp
from jax import lax
from jax.experimental import pallas as pl
from jax.experimental.pallas import tpu as pltpu
from jax.sharding import PartitionSpec as P

LEVELS = 16
KNOTS = 17
PYR = 6

SUB = 8
LANES = 128
RIM = 128
FIRST = 2
STACK = FIRST + LEVELS

VMEM = pl.BlockSpec(memory_space=pltpu.VMEM)
HBM = pl.BlockSpec(memory_space=pltpu.HBM)
PARAMS = pltpu.CompilerParams(vmem_limit_bytes=20 * 1024 * 1024)


def iota(shape, dim):
    return lax.broadcasted_iota(jnp.int32, shape, dim)


def down_taps(distance):
    size = jnp.abs(distance)
    value = jnp.where(size == 0, 6.0, jnp.where(size == 1, 4.0, jnp.where(size == 2, 1.0, 0.0)))
    return (value / 256.0).astype(jnp.bfloat16)


def up_taps(distance):
    size = jnp.abs(distance)
    value = jnp.where(size == 0, 0.75, jnp.where(size == 1, 0.5, jnp.where(size == 2, 0.125, 0.0)))
    return (value / 8.0).astype(jnp.bfloat16)


def twice(table):
    return jnp.concatenate([table, table], axis=0)


def halves(x):
    high = x.astype(jnp.bfloat16)
    low = (x - high.astype(jnp.float32)).astype(jnp.bfloat16)
    return jnp.concatenate([high, low], axis=-1)


def dot(x, table):
    return jnp.dot(x, table, preferred_element_type=jnp.float32)


def shift_down(x):
    return pltpu.roll(x, 1, axis=x.ndim - 2)


def shift_up(x):
    return pltpu.roll(x, SUB - 1, axis=x.ndim - 2)


def sublane(x):
    return iota(x.shape, x.ndim - 2)


def rows_down(planes, scaled=False):
    first, last = planes[0], planes[-1]
    top = sublane(first) == 0
    quad = (lambda x: x) if scaled else (lambda x: 4.0 * x)
    minus2 = jnp.where(top, first, shift_down(planes[-2]))
    minus1 = jnp.where(top, 4.0 * first if scaled else first, shift_down(last))
    plus = jnp.where(sublane(first) == SUB - 1, 0.25 * last if scaled else last, shift_up(first))
    padded = [minus2, minus1] + list(planes) + [plus]
    out = []
    for at in range(0, len(planes), 2):
        a, b, c, d, e = padded[at:at + 5]
        out.append((a + e) + quad(b + d) + 6.0 * c)
    return out


def padded_for_up(planes):
    first, last = planes[0], planes[-1]
    below = jnp.where(sublane(first) == 0, first, shift_down(last))
    above = jnp.where(sublane(first) == SUB - 1, last, shift_up(first))
    return [below] + list(planes) + [above]


def rows_up(planes):
    padded = padded_for_up(planes)
    out = []
    for at in range(len(planes)):
        a, b, c = padded[at:at + 3]
        out.append((a + c) + 6.0 * b)
        out.append(4.0 * (b + c))
    return out


GATHER = lax.GatherDimensionNumbers(
    offset_dims=(),
    collapsed_slice_dims=(0,),
    start_index_map=(0,),
    operand_batching_dims=(1,),
    start_indices_batching_dims=(1,),
)


def look_up(table, index):
    return lax.gather(
        table, index[..., None], GATHER, (1, 1), mode=lax.GatherScatterMode.PROMISE_IN_BOUNDS
    )


def cell(x, cells):
    scaled = x * float(cells)
    index = jnp.clip(scaled.astype(jnp.int32), 0, cells - 1)
    return index, scaled - index.astype(jnp.float32)


def curve_tables(curve_row, k):
    steps = (KNOTS - 1) // 2
    turn = steps * k // (LEVELS - 1)
    phase = (steps * k % (LEVELS - 1)) / (LEVELS - 1)
    width = curve_row.shape[-1]
    row = jnp.broadcast_to(curve_row, (SUB, width))
    offset = iota((SUB, width), 1) - iota((SUB, width), 0)

    def node(shift):
        at = jnp.where(offset == steps - turn + shift, row, 0.0)
        return jnp.sum(at, axis=1, keepdims=True)

    left, middle, right = node(-1), node(0), node(1)
    slope = middle - left
    bend = (right - middle) - slope
    start = (k / (LEVELS - 1) + middle) - phase * slope - phase * bend
    spread = lambda v: jnp.broadcast_to(v, (SUB, LANES))
    return spread(start), spread(slope), spread(bend), jnp.full((SUB, LANES), phase, jnp.float32)


def remap(tables, index, rest):
    start, slope, bend, phase = tables
    bent = jnp.maximum(rest, phase)
    return look_up(start, index) + look_up(slope, index) * rest + look_up(bend, index) * bent


def remap_pair(table_ref, first, planes, index_of, rest_of):
    even, odd = [], []
    for copy in range(2):
        start, slope, bend, phase = [table_ref[first + copy, kind] for kind in range(4)]
        even.append((start, slope, bend, phase))
        odd.append((4.0 * start, 4.0 * slope, 4.0 * bend, phase))
    mapped = [[], []]
    for p in range(planes):
        index, rest = index_of(p), rest_of(p)
        for copy in range(2):
            mapped[copy].append(remap((odd if p % 2 else even)[copy], index, rest))
    return mapped


def tone_tables(low, high):
    middle = (KNOTS - 1) // 2
    scale = middle / (LEVELS - 1)
    spread = lambda v: jnp.broadcast_to(v, (SUB, LANES))
    sub = iota((SUB, LANES), 0)

    def parts(curves, k):
        level = (sub + k).astype(jnp.float32) / (LEVELS - 1)
        left, centre, right = [spread(curves[:, at:at + 1]) for at in (middle - 1, middle, middle + 1)]
        return level + centre, scale * (right - centre), scale * (centre - left)

    def following(x, then):
        return jnp.where(sub == SUB - 1, spread(then[0:1, :]), shift_up(x))

    one, two = parts(low, 0), parts(high, LEVELS // 2)
    tables = []
    for here, then in ((one, two), (two, two)):
        base = here[0]
        tables.append((base, following(here[0], then[0]) - base, here[1] - following(here[2], then[2])))
    return tables


def tone(tables, x):
    index, rest = cell(x, LEVELS - 1)
    lower = index < SUB
    place = index & (SUB - 1)
    base, step, arc = [
        jnp.where(lower, look_up(one, place), look_up(two, place)) for one, two in zip(*tables)
    ]
    return base + rest * (step + (1.0 - rest) * arc)


def scaled_level(x):
    place = x * float(LEVELS - 1)
    half = 0.5 * place
    return place, jnp.abs(1.0 - 2.0 * (half - jnp.floor(half)))


def stage_kernel(image_ref, whole_ref, edge_ref, own_ref, rim_ref, wide_ref, small_ref, full_ref,
                 narrow_ref, sems):
    lvl = lax.axis_index("lvl")
    tiles = whole_ref.shape[0]
    start = pl.multiple_of(lvl * (tiles - 1) * LANES, LANES)
    copies = [pltpu.make_async_copy(image_ref.at[:, pl.ds(start, RIM)], edge_ref, sems.at[tiles])]
    for tile in range(tiles):
        source = image_ref.at[:, tile * LANES:(tile + 1) * LANES]
        copies.append(pltpu.make_async_copy(source, whole_ref.at[tile], sems.at[tile]))
    for copy in copies:
        copy.start()

    half = tiles * LANES // 2

    def put(ref, shape, value):
        table = value(iota(shape, 0), iota(shape, 1))
        ref[0:shape[0], :] = table
        ref[shape[0]:2 * shape[0], :] = table

    inner = jnp.where(lvl == 1, half + RIM, 0)
    outer = jnp.where(lvl == 0, -RIM, half)
    put(own_ref, (half + RIM, half),
        lambda i, j: down_taps(jnp.where(i >= half, i - inner, i) - 2 * (j - RIM // 2)))
    put(rim_ref, (RIM, LANES), lambda i, j: down_taps(i + outer - 2 * (j + lvl * LANES - RIM // 2)))
    put(wide_ref, (half, LANES), lambda i, j: down_taps(i - 2 * j))
    put(small_ref, (LANES, LANES), lambda i, j: down_taps(i - 2 * j))
    put(full_ref, (half, half), lambda i, j: up_taps(2 * i - (j + RIM)))
    put(narrow_ref, (LANES, half), lambda i, j: up_taps(2 * i - j))
    for copy in copies:
        copy.wait()


def put_kernel(half_ref, out_ref, sems, lvl):
    tiles = half_ref.shape[0]
    copies = []
    for tile in range(tiles):
        start = pl.multiple_of((lvl * tiles + tile) * LANES, LANES)
        target = out_ref.at[:, pl.ds(start, LANES)]
        copies.append(pltpu.make_async_copy(half_ref.at[tile], target, sems.at[tile]))
    for copy in copies:
        copy.start()
    for copy in copies:
        copy.wait()


def put_mine_kernel(mine_ref, out_ref, sems):
    put_kernel(mine_ref, out_ref, sems, lax.axis_index("lvl"))


def put_theirs_kernel(theirs_ref, begun_ref, out_ref, sems):
    put_kernel(theirs_ref, out_ref, sems, 1 - lax.axis_index("lvl"))


def pick(place, weight, values):
    even, odd = values(0), values(1)
    for k in range(2, LEVELS, 2):
        even = jnp.where(place >= float(k - 1), values(k), even)
        odd = jnp.where(place >= float(k), values(k + 1), odd)
    return odd + weight * (even - odd)


def split_store(ref, reduced, column, width):
    for pair in range(len(reduced) // 2):
        both = jnp.concatenate(reduced[2 * pair:2 * pair + 2], axis=0)
        high = both.astype(jnp.bfloat16)
        low = (both - high.astype(jnp.float32)).astype(jnp.bfloat16)
        ref[pair, :, column:column + LANES] = high
        ref[pair, :, width + column:width + column + LANES] = low


def scale_odd(planes):
    return [4.0 * x if p % 2 else x for p, x in enumerate(planes)]


def own_kernel(image_ref, mine_ref, other_ref, down_ref, gauss_ref, tone_ref, place_ref, weight_ref,
               table_ref, x_scr, cell_scr, rest_scr, part_scr):
    lvl = lax.axis_index("lvl")
    tiles, rows, _ = image_ref.shape
    planes = rows // SUB
    half = tiles * LANES // 2
    own = half + RIM
    pairs = LEVELS // 2

    first = jnp.where(lvl == 0, mine_ref[...], other_ref[...])
    second = jnp.where(lvl == 0, other_ref[...], mine_ref[...])
    for k in range(LEVELS):
        source = first if k < pairs else second
        row = k % pairs
        for kind, table in enumerate(curve_tables(source[row:row + 1, :], k)):
            table_ref[k, kind] = table
    tones = tone_tables(first, second)

    sources = [lvl * (tiles // 2) + tile for tile in range(tiles // 2)] + [tiles // 2 - lvl]
    for tile, source in enumerate(sources):
        span = slice(tile * LANES, (tile + 1) * LANES)
        for p in range(planes):
            x = image_ref[source, pl.ds(p, SUB, stride=planes), :]
            x_scr[p, :, span] = x
            cell_scr[p, :, span], rest_scr[p, :, span] = cell(x, (KNOTS - 1) // 2)
            if tile < tiles // 2:
                tone_ref[p, :, span] = tone(tones, x)
                place_ref[p, :, span], weight_ref[p, :, span] = scaled_level(x)

    def multiply(slot, target):
        part = part_scr[slot].reshape(-1, 2 * own)
        result = dot(part, down_ref[...]).reshape(2, planes // 4, 2, SUB, half)
        for copy in range(2):
            for tile in range(half // LANES):
                span = slice(tile * LANES, (tile + 1) * LANES)
                gauss_ref[tile, :, target + copy] = result[copy, :, :, :, span]

    for column in range(0, own, LANES):
        guide = scale_odd([x_scr[p, :, column:column + LANES] for p in range(planes)])
        reduced = rows_down(guide, scaled=True)
        for copy in range(2):
            split_store(part_scr.at[1, copy], reduced, column, own)

    def one_pair(step, carry):
        slot = lax.rem(step, 2)
        multiply(1 - slot, 2 * step)
        for column in range(0, own, LANES):
            span = slice(column, column + LANES)
            mapped = remap_pair(
                table_ref, 2 * step, planes, lambda p: cell_scr[p, :, span], lambda p: rest_scr[p, :, span]
            )
            for copy in range(2):
                split_store(part_scr.at[slot, copy], rows_down(mapped[copy], scaled=True), column, own)
        return carry

    lax.fori_loop(0, pairs, one_pair, 0)
    multiply((pairs - 1) % 2, 2 * pairs)


def rest_kernel(halo_ref, gauss_in_ref, tone_ref, place_ref, weight_ref, table_ref, rim_ref, wide_ref,
                small_ref, full_ref, narrow_ref, out_ref, gauss_ref, x_scr, cell_scr, rest_scr, part_scr,
                up_scr):
    lvl = lax.axis_index("lvl")
    rows = halo_ref.shape[0]
    planes = rows // SUB
    tiles = out_ref.shape[0]
    half = tiles * LANES
    pairs = LEVELS // 2

    for p in range(planes):
        x = halo_ref[pl.ds(p, SUB, stride=planes), :]
        x_scr[p] = x
        cell_scr[p], rest_scr[p] = cell(x, (KNOTS - 1) // 2)

    def multiply(slot, target):
        part = part_scr[slot].reshape(-1, 2 * RIM)
        result = dot(part, rim_ref[...]).reshape(2, planes // 4, 2, SUB, LANES)
        for copy in range(2):
            gauss_ref[lvl, :, target + copy] = gauss_in_ref[lvl, :, target + copy] + result[copy]

    reduced = rows_down(scale_odd([x_scr[p] for p in range(planes)]), scaled=True)
    for copy in range(2):
        split_store(part_scr.at[1, copy], reduced, 0, RIM)

    def one_pair(step, carry):
        slot = lax.rem(step, 2)
        multiply(1 - slot, 2 * step)
        mapped = remap_pair(table_ref, 2 * step, planes, lambda p: cell_scr[p], lambda p: rest_scr[p])
        for copy in range(2):
            split_store(part_scr.at[slot, copy], rows_down(mapped[copy], scaled=True), 0, RIM)
        return carry

    lax.fori_loop(0, pairs, one_pair, 0)
    multiply((pairs - 1) % 2, 2 * pairs)

    def level_one(p, start=0):
        parts = [gauss_ref[tile, p // 2, start:, p % 2] for tile in range(tiles)]
        return jnp.concatenate(parts, axis=-1)

    source = jnp.concatenate([level_one(p, FIRST) for p in range(planes // 2)], axis=0)
    up_scr[...] = dot(halves(source.reshape(-1, half)), full_ref[...]).reshape(up_scr.shape)

    gauss = [None, [level_one(p) for p in range(planes // 2)]]
    for level in range(1, PYR - 1):
        reduced = rows_down(gauss[level])
        count = len(reduced)
        stacked = jnp.concatenate(reduced, axis=0)
        stacked = stacked.reshape(-1, stacked.shape[-1])
        result = dot(halves(stacked), (wide_ref if level == 1 else small_ref)[...])
        result = result.reshape(count, STACK, SUB, LANES)
        gauss.append([result[p] for p in range(count)])

    out = [gauss[PYR - 1][0][0]]
    for level in range(PYR - 2, 0, -1):
        columns = half if level == 1 else LANES
        table = narrow_ref[:, 0:columns]
        coarse = gauss[level + 1]
        count = len(coarse)
        stacked = jnp.concatenate([plane[FIRST:] for plane in coarse], axis=0).reshape(-1, LANES)
        wider = dot(halves(stacked), table).reshape(count, LEVELS, SUB, columns)
        raised = rows_up([wider[p] for p in range(count)])
        base = dot(halves(jnp.concatenate(out, axis=0)), table).reshape(count, SUB, columns)
        base = rows_up([base[p] for p in range(count)])
        out = []
        for p in range(2 * count):
            here = gauss[level][p]
            place, weight = scaled_level(here[0])
            out.append(pick(place, weight, lambda k: here[FIRST + k] - raised[p][k]) + base[p])

    base = dot(halves(jnp.concatenate(out, axis=0)), full_ref[...]).reshape(planes // 2, SUB, half)
    base = rows_up([base[p] for p in range(planes // 2)])
    padded = padded_for_up([up_scr[p] for p in range(planes // 2)])
    for p in range(planes):
        a, b, c = padded[p // 2], padded[p // 2 + 1], padded[p // 2 + 2]
        if p % 2 == 0:
            detail = pick(place_ref[p], weight_ref[p], lambda k: (a[k] + c[k]) + 6.0 * b[k])
        else:
            detail = 4.0 * pick(place_ref[p], weight_ref[p], lambda k: b[k] + c[k])
        toned = (tone_ref[p] - detail) + base[p]
        for tile in range(tiles):
            out_ref[tile, pl.ds(p, SUB, stride=planes), :] = toned[:, tile * LANES:(tile + 1) * LANES]


def call(kernel, name, in_specs, out_shape, scratch, out_space=VMEM, **others):
    return pl.pallas_call(
        kernel,
        name=name,
        in_specs=in_specs,
        out_specs=jax.tree.map(lambda _: out_space, out_shape),
        out_shape=out_shape,
        scratch_shapes=scratch,
        compiler_params=PARAMS,
        **others,
    )


def body(image, curves):
    rows, width = image.shape
    half = width // 2
    own = half + RIM
    planes = rows // SUB
    tiles = half // LANES
    lvl = lax.axis_index("lvl")
    count = lax.axis_size("tile")
    f32 = lambda *shape: jax.ShapeDtypeStruct(shape, jnp.float32)
    b16 = lambda *shape: jax.ShapeDtypeStruct(shape, jnp.bfloat16)
    fast = lambda *shape: pltpu.VMEM(shape, jnp.float32)
    fast_int = lambda *shape: pltpu.VMEM(shape, jnp.int32)
    fast_half = lambda *shape: pltpu.VMEM(shape, jnp.bfloat16)
    swap = [(0, 1), (1, 0)]

    other_curves = lax.ppermute(curves, "lvl", swap)
    whole, edge, down, rim, wide, small, full, narrow = call(
        stage_kernel, "stage", [HBM],
        [f32(2 * tiles, rows, LANES), f32(rows, RIM), b16(2 * own, half), b16(2 * RIM, LANES),
         b16(2 * half, LANES), b16(2 * LANES, LANES), b16(2 * half, half), b16(2 * LANES, half)],
        [pltpu.SemaphoreType.DMA((2 * tiles + 1,))],
    )(pltpu.with_memory_space_constraint(image, pltpu.HBM))
    edge, other_curves = lax.optimization_barrier((edge, other_curves))
    pairs = []
    for tile in range(count):
        pairs.append((2 * tile + 1, 2 * ((tile + 1) % count)))
        pairs.append((2 * tile, 2 * ((tile - 1) % count) + 1))
    halo = lax.ppermute(edge, ("tile", "lvl"), pairs)

    gauss_shape = f32(tiles, planes // 4, STACK, 2, SUB, LANES)
    gauss, toned, place, weight, tables = call(
        own_kernel, "own", [VMEM] * 4,
        [gauss_shape, f32(planes, SUB, half), f32(planes, SUB, half), f32(planes, SUB, half),
         f32(LEVELS, 4, SUB, LANES)],
        [fast(planes, SUB, own), fast_int(planes, SUB, own), fast(planes, SUB, own),
         fast_half(2, 2, planes // 4, 2 * SUB, 2 * own)],
    )(whole, curves, other_curves, down)
    mine, _ = call(
        rest_kernel, "rest", [VMEM] * 11, [f32(tiles, rows, LANES), gauss_shape],
        [fast(planes, SUB, RIM), fast_int(planes, SUB, RIM), fast(planes, SUB, RIM),
         fast_half(2, 2, planes // 4, 2 * SUB, 2 * RIM), fast(planes // 2, LEVELS, SUB, half)],
        input_output_aliases={1: 1},
    )(halo, gauss, toned, place, weight, tables, rim, wide, small, full, narrow)
    theirs = lax.ppermute(mine, "lvl", swap)
    sems = [pltpu.SemaphoreType.DMA((tiles,))]
    begun = call(put_mine_kernel, "put_mine", [VMEM], f32(rows, width), sems, HBM)(mine)
    return call(
        put_theirs_kernel, "put_theirs", [VMEM, HBM], f32(rows, width), sems, HBM, input_output_aliases={1: 0}
    )(theirs, begun)


def solution(mesh):
    placed = (P("band", "tile"), P("lvl", None))
    return jax.shard_map(
        body, mesh=mesh, in_specs=placed, out_specs=P("band", "tile"), check_vma=False
    )
```

time: 22.3 us -> 20.2 us (0.906)
  Pallas kernels: 13.3 us -> 12.2 us
  local copies, waits for them, and re-layouts: 1.73 us -> 0.69 us
    unnamed x4 -> x2, local copies, waits for them, and re-layouts: 1.73 us -> 0.69 us
    pallas_call x3, Pallas kernels: 11.8 us -> 10.8 us  [the longest x1 4.87 us: body(): call(rest_kernel, 'rest', [VMEM] * 11, [f32(tiles, rows, LANES), gauss_sh...]
  transfers between devices with their start and end apart: 3 -> 3, of which waited for: 1 -> 1; matrix products, arithmetic and copies ran while one was open for 0% -> 0% of each run, Pallas kernels for 31% -> 33%
where the time goes in v1:
time: 20.2 us; the launch traced here: 20 us
  Pallas kernels  12.2 us (60%)
  starting transfers between devices  6.26 us (31%)
  waiting for transfers between devices  0.8 us (4%)
  local copies, waits for them, and re-layouts  0.69 us (3%)
    ppermute x1, starting transfers between devices, body(): halo = lax.ppermute(edge, ('tile', 'lvl'), pairs)  5.73 us
    pallas_call x1, Pallas kernels, body(): call(rest_kernel, 'rest', [VMEM] * 11, [f32(tiles, rows, LANES), gauss_sh...  4.87 us
    pallas_call x1, Pallas kernels, body(): call(own_kernel, 'own', [VMEM] * 4, [gauss_shape, f32(planes, SUB, half),...  4.68 us
    pallas_call x1, Pallas kernels, body(): call(stage_kernel, 'stage', [HBM], [f32(2 * tiles, rows, LANES), f32(rows...  1.22 us
    ppermute x1, waiting for transfers between devices, body(): theirs = lax.ppermute(mine, 'lvl', swap)  0.79 us
    pallas_call x1, Pallas kernels, body(): call(put_mine_kernel, 'put_mine', [VMEM], f32(rows, width), sems, HBM)(mine)  0.72 us
    pallas_call x1, Pallas kernels, body(): call(put_theirs_kernel, 'put_theirs', [VMEM, HBM], f32(rows, width), sems...  0.71 us
    unnamed x2, local copies, waits for them, and re-layouts  0.69 us
  transfers between devices with their start and end apart: 3, of which 1 were waited for; matrix products, arithmetic and copies ran while one was open for 0% of the time, Pallas kernels for 33%

profile of v1, /device:TPU:0, one launch (start us, length us, event | category | flops | bytes accessed | tf_op | source)
XLA Modules:
  0.0 20.0 jit_solution(5552177338804887452)
XLA Ops:
  0.0 0.5 %collective-permute-start = (f32[8,17]{1,0:T(8,128)}, f32[8,17]{1,0:T(8,128)S(1)}, u32[]{:S(2)}, u32[]{:S(2)}) collective-permute-start(f32[8,17]{1,0:T(8,128)} %mine_ref.1), channel_id=1, source_target_pairs={{0,1},{1,0},{2,3},{3,2},{4,5},{5,4},{6,7},{7,6},{8,9},{9,8},{10,11... | collective-permute-start | bytes 1640 | tf_op jit(solution)/shard_map/ppermute | solution.py:443
  0.5 1.2 %stage.1 = (f32[4,256,128]{2,1,0:T(8,128)S(1)}, f32[256,128]{1,0:T(8,128)S(1)}, bf16[768,256]{1,0:T(8,128)(2,1)S(1)}, bf16[256,128]{1,0:T(8,128)(2,1)S(1)}, bf16...) custom-call(f32[256,512]{1,0:T(8,128)} %image_ref.1), custom_call_target="tpu_custom_call" | custom-call | tf_op jit(solution)/shard_map/stage/pallas_call | solution.py:444
  1.7 0.0 collective-permute-done.other_ref
  1.7 5.7 %collective-permute-start.1 = (f32[256,128]{1,0:T(8,128)S(1)}, f32[256,128]{1,0:T(8,128)S(1)}, u32[]{:S(2)}, u32[]{:S(2)}) collective-permute-start(f32[256,128]{1,0:T(8,128)S(1)} %get-tuple-element.22), channel_id=1, source_target_pairs={{1,2},{0,15},{3,4},{2,1},{5,6},{4,3},{7,8},{6,5},{9,10},{8,7},{11,... | collective-permute-start | bytes 393224 | tf_op jit(solution)/shard_map/ppermute | solution.py:455
  7.4 0.0 copy-start
  7.4 0.7 %copy-done = f32[8,17]{1,0:T(8,128)S(1)} copy-done((f32[8,17]{1,0:T(8,128)S(1)}, f32[8,17]{1,0:T(8,128)}, u32[]{:S(2)}) %copy-start) | copy-done | bytes 568
  8.1 4.7 %own.1 = (f32[2,8,18,2,8,128]{5,4,3,2,1,0:T(8,128)S(1)}, f32[32,8,256]{2,1,0:T(8,128)S(1)}, f32[32,8,256]{2,1,0:T(8,128)S(1)}, f32[32,8,256]{2,1,0:T(8,128)S(1)}, f32[16,4,8,128]{3,2,1,0:T(8,128)S(1)}) custom-call(f32[4,256,128]{2,1,0:T(8,128)S(1)} %get-tuple-element.23.image_ref, f32[8,17]{1,0:T(8,128)S(1)} %copy-done, ...), custom_call_target="tpu_custom_call" | custom-call | tf_op jit(solution)/shard_map/own/pallas_call | solution.py:458
  12.8 0.0 collective-permute-done.1.halo_ref
  12.8 4.9 %rest.1 = (f32[2,256,128]{2,1,0:T(8,128)S(1)}, f32[2,8,18,2,8,128]{5,4,3,2,1,0:T(8,128)S(1)}) custom-call(f32[256,128]{1,0:T(8,128)S(1)} %collective-permute-done.1.halo_ref, f32[2,8,18,2,8,128]{5,4,3,2,1,0:T(8,128)S(1)} %get-tuple-element.26.gauss_in_ref, f32[32,8,256]{2,1,0:T(8,128)S(1)} %get-tuple-element.27.tone_ref, ...), custom_call_target="tpu_custom_call", output_to_operand_aliasing={{1}: (1, {})} | custom-call | tf_op jit(solution)/shard_map/rest/pallas_call | solution.py:465
  17.7 0.1 collective-permute-start.2
  17.8 0.7 %put_mine.1.begun_ref = f32[256,512]{1,0:T(8,128)} custom-call(f32[2,256,128]{2,1,0:T(8,128)S(1)} %get-tuple-element.36.mine_ref), custom_call_target="tpu_custom_call" | custom-call | tf_op jit(solution)/shard_map/put_mine/pallas_call | solution.py:473
  18.5 0.8 %collective-permute-done.2.theirs_ref = f32[2,256,128]{2,1,0:T(8,128)S(1)} collective-permute-done((f32[2,256,128]{2,1,0:T(8,128)S(1)}, f32[2,256,128]{2,1,0:T(8,128)S(1)}, u32[]{:S(2)}, u32[]{:S(2)}) %collective-permute-start.2) | collective-permute-done | bytes 262176 | tf_op jit(solution)/shard_map/ppermute | solution.py:471
  19.3 0.7 %put_theirs.1 = f32[256,512]{1,0:T(8,128)} custom-call(f32[2,256,128]{2,1,0:T(8,128)S(1)} %collective-permute-done.2.theirs_ref, f32[256,512]{1,0:T(8,128)} %put_mine.1.begun_ref), custom_call_target="tpu_custom_call", output_to_operand_aliasing={{}: (1, {})} | custom-call | tf_op jit(solution)/shard_map/put_theirs/pallas_call | solution.py:474
Async XLA Ops:
  0.0 1.7 %collective-permute-start = (f32[8,17]{1,0:T(8,128)}, f32[8,17]{1,0:T(8,128)S(1)}, u32[]{:S(2)}, u32[]{:S(2)}) collective-permute-start(f32[8,17]{1,0:T(8,128)} %mine_ref.1), channel_id=1, source_target_pairs={{0,1},{1,0},{2,3},{3,2},{4,5},{5,4},{6,7},{7,6},{8,9},{9,8},{10,11... | collective-permute-start | bytes 1640 | tf_op jit(solution)/shard_map/ppermute | solution.py:443
  1.7 11.1 %collective-permute-start.1 = (f32[256,128]{1,0:T(8,128)S(1)}, f32[256,128]{1,0:T(8,128)S(1)}, u32[]{:S(2)}, u32[]{:S(2)}) collective-permute-start(f32[256,128]{1,0:T(8,128)S(1)} %get-tuple-element.22), channel_id=1, source_target_pairs={{1,2},{0,15},{3,4},{2,1},{5,6},{4,3},{7,8},{6,5},{9,10},{8,7},{11,... | collective-permute-start | bytes 393224 | tf_op jit(solution)/shard_map/ppermute | solution.py:455
  7.4 0.7 %copy-start = (f32[8,17]{1,0:T(8,128)S(1)}, f32[8,17]{1,0:T(8,128)}, u32[]{:S(2)}) copy-start(f32[8,17]{1,0:T(8,128)} %mine_ref.1) | copy-start | bytes 1636
  17.7 1.6 %collective-permute-start.2 = (f32[2,256,128]{2,1,0:T(8,128)S(1)}, f32[2,256,128]{2,1,0:T(8,128)S(1)}, u32[]{:S(2)}, u32[]{:S(2)}) collective-permute-start(f32[2,256,128]{2,1,0:T(8,128)S(1)} %get-tuple-element.36.mine_ref), channel_id=1, source_target_pairs={{0,1},{1,0},{2,3},{3,2},{4,5},{5,4},{6,7},{7,6},{8,9},{9,8},{10,11... | collective-permute-start | bytes 786440 | tf_op jit(solution)/shard_map/ppermute | solution.py:471

commit v2 on v1

--- a/solution.py
+++ b/solution.py
@@ -16,6 +16,8 @@
 RIM = 128
 FIRST = 2
 STACK = FIRST + LEVELS
+FINE = (LEVELS - 1) * (KNOTS - 1) // 2
+TABLES = 11
 
 VMEM = pl.BlockSpec(memory_space=pltpu.VMEM)
 HBM = pl.BlockSpec(memory_space=pltpu.HBM)
@@ -35,11 +37,7 @@
 def up_taps(distance):
     size = jnp.abs(distance)
     value = jnp.where(size == 0, 0.75, jnp.where(size == 1, 0.5, jnp.where(size == 2, 0.125, 0.0)))
-    return (value / 8.0).astype(jnp.bfloat16)
-
-
-def twice(table):
-    return jnp.concatenate([table, table], axis=0)
+    return (value / 2.0).astype(jnp.bfloat16)
 
 
 def halves(x):
@@ -88,33 +86,42 @@
 
 def rows_up(planes):
     padded = padded_for_up(planes)
+    sums = [one + two for one, two in zip(padded[:-1], padded[1:])]
     out = []
     for at in range(len(planes)):
-        a, b, c = padded[at:at + 3]
-        out.append((a + c) + 6.0 * b)
-        out.append(4.0 * (b + c))
+        out.append(0.25 * (sums[at] + sums[at + 1]) + planes[at])
+        out.append(sums[at + 1])
     return out
 
 
-GATHER = lax.GatherDimensionNumbers(
-    offset_dims=(),
-    collapsed_slice_dims=(0,),
-    start_index_map=(0,),
-    operand_batching_dims=(1,),
-    start_indices_batching_dims=(1,),
-)
-
-
-def look_up(table, index):
+def gather_along(dim):
+    return lax.GatherDimensionNumbers(
+        offset_dims=(),
+        collapsed_slice_dims=(dim,),
+        start_index_map=(dim,),
+        operand_batching_dims=(1 - dim,),
+        start_indices_batching_dims=(1 - dim,),
+    )
+
+
+def look_up(table, index, dim=0):
     return lax.gather(
-        table, index[..., None], GATHER, (1, 1), mode=lax.GatherScatterMode.PROMISE_IN_BOUNDS
+        table, index[..., None], gather_along(dim), (1, 1), mode=lax.GatherScatterMode.PROMISE_IN_BOUNDS
     )
 
 
 def cell(x, cells):
     scaled = x * float(cells)
-    index = jnp.clip(scaled.astype(jnp.int32), 0, cells - 1)
-    return index, scaled - index.astype(jnp.float32)
+    index = jnp.minimum(jnp.floor(scaled), float(cells - 1))
+    return index.astype(jnp.int32), scaled - index
+
+
+def by_lane(p):
+    return p % 4 == 1
+
+
+def curve_cell(p, x):
+    return cell(x, FINE if by_lane(p) else (KNOTS - 1) // 2)
 
 
 def curve_tables(curve_row, k):
@@ -134,7 +141,16 @@
     bend = (right - middle) - slope
     start = (k / (LEVELS - 1) + middle) - phase * slope - phase * bend
     spread = lambda v: jnp.broadcast_to(v, (SUB, LANES))
-    return spread(start), spread(slope), spread(bend), jnp.full((SUB, LANES), phase, jnp.float32)
+    coarse = (spread(start), spread(slope), spread(bend))
+    phase = jnp.full((SUB, LANES), phase, jnp.float32)
+
+    lane = iota((SUB, LANES), 1)
+    index = jnp.minimum(jnp.floor((lane.astype(jnp.float32) + 0.5) / (LEVELS - 1)), float(SUB - 1))
+    index = index.astype(jnp.int32)
+    within = (lane - (LEVELS - 1) * index).astype(jnp.float32)
+    ends = [remap(coarse + (phase,), index, (within + side) / (LEVELS - 1)) for side in (0.0, 1.0)]
+    fine = (ends[0], ends[1] - ends[0])
+    return (phase,) + coarse + fine + tuple(4.0 * table for table in coarse + fine)
 
 
 def remap(tables, index, rest):
@@ -144,16 +160,18 @@
 
 
 def remap_pair(table_ref, first, planes, index_of, rest_of):
-    even, odd = [], []
-    for copy in range(2):
-        start, slope, bend, phase = [table_ref[first + copy, kind] for kind in range(4)]
-        even.append((start, slope, bend, phase))
-        odd.append((4.0 * start, 4.0 * slope, 4.0 * bend, phase))
+    tables = [[table_ref[first + copy, kind] for kind in range(TABLES)] for copy in range(2)]
     mapped = [[], []]
     for p in range(planes):
         index, rest = index_of(p), rest_of(p)
+        at = 6 if p % 2 else 1
         for copy in range(2):
-            mapped[copy].append(remap((odd if p % 2 else even)[copy], index, rest))
+            phase, (start, slope, bend, value, step) = tables[copy][0], tables[copy][at:at + 5]
+            if by_lane(p):
+                result = look_up(value, index, 1) + look_up(step, index, 1) * rest
+            else:
+                result = remap((start, slope, bend, phase), index, rest)
+            mapped[copy].append(result)
     return mapped
 
 
@@ -195,12 +213,15 @@
     return place, jnp.abs(1.0 - 2.0 * (half - jnp.floor(half)))
 
 
-def stage_kernel(image_ref, whole_ref, edge_ref, own_ref, rim_ref, wide_ref, small_ref, full_ref,
+def stage_kernel(image_ref, curves_ref, whole_ref, edge_ref, mine_ref, own_ref, rim_ref, wide_ref, small_ref, full_ref,
                  narrow_ref, sems):
     lvl = lax.axis_index("lvl")
     tiles = whole_ref.shape[0]
     start = pl.multiple_of(lvl * (tiles - 1) * LANES, LANES)
-    copies = [pltpu.make_async_copy(image_ref.at[:, pl.ds(start, RIM)], edge_ref, sems.at[tiles])]
+    copies = [
+        pltpu.make_async_copy(image_ref.at[:, pl.ds(start, RIM)], edge_ref, sems.at[tiles]),
+        pltpu.make_async_copy(curves_ref, mine_ref, sems.at[tiles + 1]),
+    ]
     for tile in range(tiles):
         source = image_ref.at[:, tile * LANES:(tile + 1) * LANES]
         copies.append(pltpu.make_async_copy(source, whole_ref.at[tile], sems.at[tile]))
@@ -293,7 +314,7 @@
         for p in range(planes):
             x = image_ref[source, pl.ds(p, SUB, stride=planes), :]
             x_scr[p, :, span] = x
-            cell_scr[p, :, span], rest_scr[p, :, span] = cell(x, (KNOTS - 1) // 2)
+            cell_scr[p, :, span], rest_scr[p, :, span] = curve_cell(p, x)
             if tile < tiles // 2:
                 tone_ref[p, :, span] = tone(tones, x)
                 place_ref[p, :, span], weight_ref[p, :, span] = scaled_level(x)
@@ -324,7 +345,7 @@
                 split_store(part_scr.at[slot, copy], rows_down(mapped[copy], scaled=True), column, own)
         return carry
 
-    lax.fori_loop(0, pairs, one_pair, 0)
+    lax.fori_loop(0, pairs, one_pair, 0, unroll=pairs)
     multiply((pairs - 1) % 2, 2 * pairs)
 
 
@@ -341,7 +362,7 @@
     for p in range(planes):
         x = halo_ref[pl.ds(p, SUB, stride=planes), :]
         x_scr[p] = x
-        cell_scr[p], rest_scr[p] = cell(x, (KNOTS - 1) // 2)
+        cell_scr[p], rest_scr[p] = curve_cell(p, x)
 
     def multiply(slot, target):
         part = part_scr[slot].reshape(-1, 2 * RIM)
@@ -361,7 +382,7 @@
             split_store(part_scr.at[slot, copy], rows_down(mapped[copy], scaled=True), 0, RIM)
         return carry
 
-    lax.fori_loop(0, pairs, one_pair, 0)
+    lax.fori_loop(0, pairs, one_pair, 0, unroll=pairs)
     multiply((pairs - 1) % 2, 2 * pairs)
 
     def level_one(p, start=0):
@@ -400,13 +421,15 @@
 
     base = dot(halves(jnp.concatenate(out, axis=0)), full_ref[...]).reshape(planes // 2, SUB, half)
     base = rows_up([base[p] for p in range(planes // 2)])
-    padded = padded_for_up([up_scr[p] for p in range(planes // 2)])
+    rows = [up_scr[p] for p in range(planes // 2)]
+    padded = padded_for_up(rows)
+    sums = [one + two for one, two in zip(padded[:-1], padded[1:])]
     for p in range(planes):
-        a, b, c = padded[p // 2], padded[p // 2 + 1], padded[p // 2 + 2]
+        above, below, here = sums[p // 2], sums[p // 2 + 1], rows[p // 2]
         if p % 2 == 0:
-            detail = pick(place_ref[p], weight_ref[p], lambda k: (a[k] + c[k]) + 6.0 * b[k])
+            detail = pick(place_ref[p], weight_ref[p], lambda k: 0.25 * (above[k] + below[k]) + here[k])
         else:
-            detail = 4.0 * pick(place_ref[p], weight_ref[p], lambda k: b[k] + c[k])
+            detail = pick(place_ref[p], weight_ref[p], lambda k: below[k])
         toned = (tone_ref[p] - detail) + base[p]
         for tile in range(tiles):
             out_ref[tile, pl.ds(p, SUB, stride=planes), :] = toned[:, tile * LANES:(tile + 1) * LANES]
@@ -441,12 +464,12 @@
     swap = [(0, 1), (1, 0)]
 
     other_curves = lax.ppermute(curves, "lvl", swap)
-    whole, edge, down, rim, wide, small, full, narrow = call(
-        stage_kernel, "stage", [HBM],
-        [f32(2 * tiles, rows, LANES), f32(rows, RIM), b16(2 * own, half), b16(2 * RIM, LANES),
+    whole, edge, mine, down, rim, wide, small, full, narrow = call(
+        stage_kernel, "stage", [HBM] * 2,
+        [f32(2 * tiles, rows, LANES), f32(rows, RIM), f32(*curves.shape), b16(2 * own, half), b16(2 * RIM, LANES),
          b16(2 * half, LANES), b16(2 * LANES, LANES), b16(2 * half, half), b16(2 * LANES, half)],
-        [pltpu.SemaphoreType.DMA((2 * tiles + 1,))],
-    )(pltpu.with_memory_space_constraint(image, pltpu.HBM))
+        [pltpu.SemaphoreType.DMA((2 * tiles + 2,))],
+    )(pltpu.with_memory_space_constraint(image, pltpu.HBM), pltpu.with_memory_space_constraint(curves, pltpu.HBM))
     edge, other_curves = lax.optimization_barrier((edge, other_curves))
     pairs = []
     for tile in range(count):
@@ -458,10 +481,10 @@
     gauss, toned, place, weight, tables = call(
         own_kernel, "own", [VMEM] * 4,
         [gauss_shape, f32(planes, SUB, half), f32(planes, SUB, half), f32(planes, SUB, half),
-         f32(LEVELS, 4, SUB, LANES)],
+         f32(LEVELS, TABLES, SUB, LANES)],
         [fast(planes, SUB, own), fast_int(planes, SUB, own), fast(planes, SUB, own),
          fast_half(2, 2, planes // 4, 2 * SUB, 2 * own)],
-    )(whole, curves, other_curves, down)
+    )(whole, mine, other_curves, down)
     mine, _ = call(
         rest_kernel, "rest", [VMEM] * 11, [f32(tiles, rows, LANES), gauss_shape],
         [fast(planes, SUB, RIM), fast_int(planes, SUB, RIM), fast(planes, SUB, RIM),

time: 20.2 us -> 17.7 us (0.88)
  Pallas kernels: 12.2 us -> 10.5 us
  local copies, waits for them, and re-layouts: 0.69 us -> 0 us
    pallas_call x1, Pallas kernels: 4.68 us -> 3.69 us  [body(): call(own_kernel, 'own', [VMEM] * 4, [gauss_shape, f32(planes, SUB, half),...]
    pallas_call x1, Pallas kernels: 4.87 us -> 4.13 us  [body(): call(rest_kernel, 'rest', [VMEM] * 11, [f32(tiles, rows, LANES), gauss_sh...]
    unnamed x2 -> x0, local copies, waits for them, and re-layouts: 0.69 us -> none
  transfers between devices with their start and end apart: 3 -> 3, of which waited for: 1 -> 1; matrix products, arithmetic and copies ran while one was open for 0% -> 0% of each run, Pallas kernels for 33% -> 32%
where the time goes in v2:
time: 17.7 us; the launch traced here: 17.6 us
  Pallas kernels  10.5 us (59%)
  starting transfers between devices  6.26 us (35%)
  waiting for transfers between devices  0.8 us (5%)
    ppermute x1, starting transfers between devices, body(): halo = lax.ppermute(edge, ('tile', 'lvl'), pairs)  5.73 us
    pallas_call x1, Pallas kernels, body(): call(rest_kernel, 'rest', [VMEM] * 11, [f32(tiles, rows, LANES), gauss_sh...  4.13 us
    pallas_call x1, Pallas kernels, body(): call(own_kernel, 'own', [VMEM] * 4, [gauss_shape, f32(planes, SUB, half),...  3.69 us
    pallas_call x1, Pallas kernels, body(): call(stage_kernel, 'stage', [HBM] * 2, [f32(2 * tiles, rows, LANES), f32(...  1.25 us
    ppermute x1, waiting for transfers between devices, body(): theirs = lax.ppermute(mine, 'lvl', swap)  0.79 us
    pallas_call x1, Pallas kernels, body(): call(put_mine_kernel, 'put_mine', [VMEM], f32(rows, width), sems, HBM)(mine)  0.72 us
    pallas_call x1, Pallas kernels, body(): call(put_theirs_kernel, 'put_theirs', [VMEM, HBM], f32(rows, width), sems...  0.71 us
    ppermute x1, starting transfers between devices, body(): other_curves = lax.ppermute(curves, 'lvl', swap)  0.45 us
  transfers between devices with their start and end apart: 3, of which 1 were waited for; matrix products, arithmetic and copies ran while one was open for 0% of the time, Pallas kernels for 32%

profile of v2, /device:TPU:0, one launch (start us, length us, event | category | flops | bytes accessed | tf_op | source)
XLA Modules:
  0.0 17.6 jit_solution(2740935652078484667)
XLA Ops:
  0.0 0.5 %collective-permute-start = (f32[8,17]{1,0:T(8,128)}, f32[8,17]{1,0:T(8,128)S(1)}, u32[]{:S(2)}, u32[]{:S(2)}) collective-permute-start(f32[8,17]{1,0:T(8,128)} %curves_ref.1), channel_id=1, source_target_pairs={{0,1},{1,0},{2,3},{3,2},{4,5},{5,4},{6,7},{7,6},{8,9},{9,8},{10,11... | collective-permute-start | bytes 1640 | tf_op jit(solution)/shard_map/ppermute | solution.py:466
  0.5 1.2 %stage.1 = (f32[4,256,128]{2,1,0:T(8,128)S(1)}, f32[256,128]{1,0:T(8,128)S(1)}, f32[8,17]{1,0:T(8,128)S(1)}, bf16[768,256]{1,0:T(8,128)(2,1)S(1)}, bf16[256,128]...) custom-call(f32[256,512]{1,0:T(8,128)} %image_ref.1, ...), custom_call_target="tpu_custom_call" | custom-call | tf_op jit(solution)/shard_map/stage/pallas_call | solution.py:467
  1.7 0.0 collective-permute-done.other_ref
  1.7 5.7 %collective-permute-start.1 = (f32[256,128]{1,0:T(8,128)S(1)}, f32[256,128]{1,0:T(8,128)S(1)}, u32[]{:S(2)}, u32[]{:S(2)}) collective-permute-start(f32[256,128]{1,0:T(8,128)S(1)} %get-tuple-element.23), channel_id=1, source_target_pairs={{1,2},{0,15},{3,4},{2,1},{5,6},{4,3},{7,8},{6,5},{9,10},{8,7},{11,... | collective-permute-start | bytes 393224 | tf_op jit(solution)/shard_map/ppermute | solution.py:478
  7.5 3.7 %own.1 = (f32[2,8,18,2,8,128]{5,4,3,2,1,0:T(8,128)S(1)}, f32[32,8,256]{2,1,0:T(8,128)S(1)}, f32[32,8,256]{2,1,0:T(8,128)S(1)}, f32[32,8,256]{2,1,0:T(8,128)S(1)}, f32[16,11,8,128]{3,2,1,0:T(8,128)S(1)}) custom-call(f32[4,256,128]{2,1,0:T(8,128)S(1)} %get-tuple-element.24.image_ref, f32[8,17]{1,0:T(8,128)S(1)} %get-tuple-element.25.mine_ref, ...), custom_call_target="tpu_custom_call" | custom-call | tf_op jit(solution)/shard_map/own/pallas_call | solution.py:481
  11.1 0.0 collective-permute-done.1.halo_ref
  11.2 4.1 %rest.1 = (f32[2,256,128]{2,1,0:T(8,128)S(1)}, f32[2,8,18,2,8,128]{5,4,3,2,1,0:T(8,128)S(1)}) custom-call(f32[256,128]{1,0:T(8,128)S(1)} %collective-permute-done.1.halo_ref, f32[2,8,18,2,8,128]{5,4,3,2,1,0:T(8,128)S(1)} %get-tuple-element.28.gauss_in_ref, f32[32,8,256]{2,1,0:T(8,128)S(1)} %get-tuple-element.29.tone_ref, ...), custom_call_target="tpu_custom_call", output_to_operand_aliasing={{1}: (1, {})} | custom-call | tf_op jit(solution)/shard_map/rest/pallas_call | solution.py:488
  15.3 0.1 collective-permute-start.2
  15.4 0.7 %put_mine.1.begun_ref = f32[256,512]{1,0:T(8,128)} custom-call(f32[2,256,128]{2,1,0:T(8,128)S(1)} %get-tuple-element.38.mine_ref), custom_call_target="tpu_custom_call" | custom-call | tf_op jit(solution)/shard_map/put_mine/pallas_call | solution.py:496
  16.1 0.8 %collective-permute-done.2.theirs_ref = f32[2,256,128]{2,1,0:T(8,128)S(1)} collective-permute-done((f32[2,256,128]{2,1,0:T(8,128)S(1)}, f32[2,256,128]{2,1,0:T(8,128)S(1)}, u32[]{:S(2)}, u32[]{:S(2)}) %collective-permute-start.2) | collective-permute-done | bytes 262176 | tf_op jit(solution)/shard_map/ppermute | solution.py:494
  16.9 0.7 %put_theirs.1 = f32[256,512]{1,0:T(8,128)} custom-call(f32[2,256,128]{2,1,0:T(8,128)S(1)} %collective-permute-done.2.theirs_ref, f32[256,512]{1,0:T(8,128)} %put_mine.1.begun_ref), custom_call_target="tpu_custom_call", output_to_operand_aliasing={{}: (1, {})} | custom-call | tf_op jit(solution)/shard_map/put_theirs/pallas_call | solution.py:497
Async XLA Ops:
  0.0 1.7 %collective-permute-start = (f32[8,17]{1,0:T(8,128)}, f32[8,17]{1,0:T(8,128)S(1)}, u32[]{:S(2)}, u32[]{:S(2)}) collective-permute-start(f32[8,17]{1,0:T(8,128)} %curves_ref.1), channel_id=1, source_target_pairs={{0,1},{1,0},{2,3},{3,2},{4,5},{5,4},{6,7},{7,6},{8,9},{9,8},{10,11... | collective-permute-start | bytes 1640 | tf_op jit(solution)/shard_map/ppermute | solution.py:466
  1.7 9.4 %collective-permute-start.1 = (f32[256,128]{1,0:T(8,128)S(1)}, f32[256,128]{1,0:T(8,128)S(1)}, u32[]{:S(2)}, u32[]{:S(2)}) collective-permute-start(f32[256,128]{1,0:T(8,128)S(1)} %get-tuple-element.23), channel_id=1, source_target_pairs={{1,2},{0,15},{3,4},{2,1},{5,6},{4,3},{7,8},{6,5},{9,10},{8,7},{11,... | collective-permute-start | bytes 393224 | tf_op jit(solution)/shard_map/ppermute | solution.py:478
  15.3 1.6 %collective-permute-start.2 = (f32[2,256,128]{2,1,0:T(8,128)S(1)}, f32[2,256,128]{2,1,0:T(8,128)S(1)}, u32[]{:S(2)}, u32[]{:S(2)}) collective-permute-start(f32[2,256,128]{2,1,0:T(8,128)S(1)} %get-tuple-element.38.mine_ref), channel_id=1, source_target_pairs={{0,1},{1,0},{2,3},{3,2},{4,5},{5,4},{6,7},{7,6},{8,9},{9,8},{10,11... | collective-permute-start | bytes 786440 | tf_op jit(solution)/shard_map/ppermute | solution.py:494

commit v3 on v2

v3 whole, which is shorter than its diff:
```python
import functools

import jax
import jax.numpy as jnp
from jax import lax
from jax.experimental import pallas as pl
from jax.experimental.pallas import tpu as pltpu
from jax.sharding import PartitionSpec as P

LEVELS = 16
KNOTS = 17
PYR = 6

SUB = 8
LANES = 128
RIM = LANES
FIRST = 2
STACK = FIRST + LEVELS
LEFT, RIGHT = 2, 126
FINE = (LEVELS - 1) * (KNOTS - 1) // 2
TABLES = 11

VMEM = pl.BlockSpec(memory_space=pltpu.VMEM)
HBM = pl.BlockSpec(memory_space=pltpu.HBM)
PARAMS = pltpu.CompilerParams(vmem_limit_bytes=20 * 1024 * 1024)


def iota(shape, dim):
    return lax.broadcasted_iota(jnp.int32, shape, dim)


def down_taps(distance):
    size = jnp.abs(distance)
    value = jnp.where(size == 0, 6.0, jnp.where(size == 1, 4.0, jnp.where(size == 2, 1.0, 0.0)))
    return (value / 256.0).astype(jnp.bfloat16)


def up_taps(distance):
    size = jnp.abs(distance)
    value = jnp.where(size == 0, 0.75, jnp.where(size == 1, 0.5, jnp.where(size == 2, 0.125, 0.0)))
    return (value / 2.0).astype(jnp.bfloat16)


def halves(x):
    high = x.astype(jnp.bfloat16)
    low = (x - high.astype(jnp.float32)).astype(jnp.bfloat16)
    return jnp.concatenate([high, low], axis=-1)


def dot(x, table):
    return jnp.dot(x, table, preferred_element_type=jnp.float32)


def shift_down(x):
    return pltpu.roll(x, 1, axis=x.ndim - 2)


def shift_up(x):
    return pltpu.roll(x, SUB - 1, axis=x.ndim - 2)


def sublane(x):
    return iota(x.shape, x.ndim - 2)


def rows_down(planes, scaled=False):
    first, last = planes[0], planes[-1]
    top = sublane(first) == 0
    quad = (lambda x: x) if scaled else (lambda x: 4.0 * x)
    minus2 = jnp.where(top, first, shift_down(planes[-2]))
    minus1 = jnp.where(top, 4.0 * first if scaled else first, shift_down(last))
    plus = jnp.where(sublane(first) == SUB - 1, 0.25 * last if scaled else last, shift_up(first))
    padded = [minus2, minus1] + list(planes) + [plus]
    out = []
    for at in range(0, len(planes), 2):
        a, b, c, d, e = padded[at:at + 5]
        out.append((a + e) + quad(b + d) + 6.0 * c)
    return out


def padded_for_up(planes):
    first, last = planes[0], planes[-1]
    below = jnp.where(sublane(first) == 0, first, shift_down(last))
    above = jnp.where(sublane(first) == SUB - 1, last, shift_up(first))
    return [below] + list(planes) + [above]


def rows_up(planes):
    padded = padded_for_up(planes)
    sums = [one + two for one, two in zip(padded[:-1], padded[1:])]
    out = []
    for at in range(len(planes)):
        out.append(0.25 * (sums[at] + sums[at + 1]) + planes[at])
        out.append(sums[at + 1])
    return out


def gather_along(dim):
    return lax.GatherDimensionNumbers(
        offset_dims=(),
        collapsed_slice_dims=(dim,),
        start_index_map=(dim,),
        operand_batching_dims=(1 - dim,),
        start_indices_batching_dims=(1 - dim,),
    )


def look_up(table, index, dim=0):
    return lax.gather(
        table, index[..., None], gather_along(dim), (1, 1), mode=lax.GatherScatterMode.PROMISE_IN_BOUNDS
    )


def cell(x, cells):
    scaled = x * float(cells)
    index = jnp.minimum(jnp.floor(scaled), float(cells - 1))
    return index.astype(jnp.int32), scaled - index


def by_lane(p):
    return p % 4 == 1


def curve_cell(p, x):
    return cell(x, FINE if by_lane(p) else (KNOTS - 1) // 2)


def curve_tables(curve_row, k):
    steps = (KNOTS - 1) // 2
    turn = steps * k // (LEVELS - 1)
    phase = (steps * k % (LEVELS - 1)) / (LEVELS - 1)
    width = curve_row.shape[-1]
    row = jnp.broadcast_to(curve_row, (SUB, width))
    offset = iota((SUB, width), 1) - iota((SUB, width), 0)

    def node(shift):
        at = jnp.where(offset == steps - turn + shift, row, 0.0)
        return jnp.sum(at, axis=1, keepdims=True)

    left, middle, right = node(-1), node(0), node(1)
    slope = middle - left
    bend = (right - middle) - slope
    start = (k / (LEVELS - 1) + middle) - phase * slope - phase * bend
    spread = lambda v: jnp.broadcast_to(v, (SUB, LANES))
    coarse = (spread(start), spread(slope), spread(bend))
    phase = jnp.full((SUB, LANES), phase, jnp.float32)

    lane = iota((SUB, LANES), 1)
    index = jnp.minimum(jnp.floor((lane.astype(jnp.float32) + 0.5) / (LEVELS - 1)), float(SUB - 1))
    index = index.astype(jnp.int32)
    within = (lane - (LEVELS - 1) * index).astype(jnp.float32)
    ends = [remap(coarse + (phase,), index, (within + side) / (LEVELS - 1)) for side in (0.0, 1.0)]
    fine = (ends[0], ends[1] - ends[0])
    return (phase,) + coarse + fine + tuple(4.0 * table for table in coarse + fine)


def remap(tables, index, rest):
    start, slope, bend, phase = tables
    bent = jnp.maximum(rest, phase)
    return look_up(start, index) + look_up(slope, index) * rest + look_up(bend, index) * bent


def remap_pair(table_ref, first, planes, index_of, rest_of):
    tables = [[table_ref[first + copy, kind] for kind in range(TABLES)] for copy in range(2)]
    mapped = [[], []]
    for p in range(planes):
        index, rest = index_of(p), rest_of(p)
        at = 6 if p % 2 else 1
        for copy in range(2):
            phase, (start, slope, bend, value, step) = tables[copy][0], tables[copy][at:at + 5]
            if by_lane(p):
                result = look_up(value, index, 1) + look_up(step, index, 1) * rest
            else:
                result = remap((start, slope, bend, phase), index, rest)
            mapped[copy].append(result)
    return mapped


def tone_tables(low, high):
    middle = (KNOTS - 1) // 2
    scale = middle / (LEVELS - 1)
    spread = lambda v: jnp.broadcast_to(v, (SUB, LANES))
    sub = iota((SUB, LANES), 0)

    def parts(curves, k):
        level = (sub + k).astype(jnp.float32) / (LEVELS - 1)
        left, centre, right = [spread(curves[:, at:at + 1]) for at in (middle - 1, middle, middle + 1)]
        return level + centre, scale * (right - centre), scale * (centre - left)

    def following(x, then):
        return jnp.where(sub == SUB - 1, spread(then[0:1, :]), shift_up(x))

    one, two = parts(low, 0), parts(high, LEVELS // 2)
    lane = iota((SUB, LANES), 1)
    tables = []
    for kind in range(3):
        rows = []
        for here, then in ((one, two), (two, two)):
            if kind == 0:
                rows.append(here[0])
            elif kind == 1:
                rows.append(following(here[0], then[0]) - here[0])
            else:
                rows.append(here[1] - following(here[2], then[2]))
        along = jnp.where(lane == sub, rows[0], jnp.where(lane == sub + SUB, rows[1], 0.0))
        tables.append(spread(jnp.sum(along, axis=0, keepdims=True)))
    return tables


def tone(tables, x):
    index, rest = cell(x, LEVELS - 1)
    base, step, arc = [look_up(table, index, 1) for table in tables]
    return base + rest * (step + (1.0 - rest) * arc)


def scaled_level(x):
    place = x * float(LEVELS - 1)
    half = 0.5 * place
    return place, jnp.abs(1.0 - 2.0 * (half - jnp.floor(half)))


def start_all(pairs, sems):
    copies = [pltpu.make_async_copy(one, two, sems.at[at]) for at, (one, two) in enumerate(pairs)]
    for copy in copies:
        copy.start()
    return copies


def wait_all(copies):
    for copy in copies:
        copy.wait()


def near_column(lvl, lane):
    return lane + jnp.where(lvl == 0, LEFT, RIGHT)


def away_column(lvl, lane):
    return lane + jnp.where(lvl == 0, RIGHT, LEFT)


def level_one_column(lvl, at):
    return jnp.where(at < LANES, near_column(lvl, at), away_column(lvl, at - LANES))


def stage_kernel(image_ref, curves_ref, edge_ref, inner_ref, mine_ref, own_ref, rim_ref, wide_ref,
                 small_ref, near_ref, away_ref, narrow_ref, raise_ref, sems):
    lvl = lax.axis_index("lvl")
    planes = edge_ref.shape[0]
    half = 2 * LANES
    outermost = pl.multiple_of(lvl * 3 * LANES, LANES)
    pairs = [(curves_ref, mine_ref)]
    for q in range(SUB):
        rows = pl.ds(q * planes, planes)
        pairs.append((image_ref.at[rows, pl.ds(outermost, LANES)], edge_ref.at[:, q, :]))
        for tile in range(2):
            source = image_ref.at[rows, (tile + 1) * LANES:(tile + 2) * LANES]
            pairs.append((source, inner_ref.at[tile, :, q, :]))
    copies = start_all(pairs, sems)

    def put(ref, shape, value):
        table = value(iota(shape, 0), iota(shape, 1))
        ref[0:shape[0], :] = table
        ref[shape[0]:2 * shape[0], :] = table

    def place(i):
        tile = i // LANES
        return jnp.where(lvl == 0, i, i - 2 * tile * LANES + LANES)

    def rim_place(i):
        return i + jnp.where(lvl == 0, -RIM, half)

    def out_place(far, j):
        return j + jnp.where(lvl == far, 0, LANES)

    def wide(i, j):
        column = level_one_column(lvl, i)
        left = (i < LANES) == (lvl == 0)
        return jnp.where(left == (j < LANES // 2), down_taps(column - 2 * j), 0.0)

    def up_pair(column, far):
        def value(i, j):
            lane = j & (LANES - 1)
            taps = up_taps(2 * column(lvl, i) - (out_place(far, lane) + RIM))
            return jnp.where(j < LANES, taps, 0.25 * taps)
        return value

    put(own_ref, (3 * LANES, half),
        lambda i, j: down_taps(place(i) - 2 * (level_one_column(lvl, j) - RIM // 2)))
    put(rim_ref, (RIM, LANES), lambda i, j: down_taps(rim_place(i) - 2 * (near_column(lvl, j) - RIM // 2)))
    put(wide_ref, (half, LANES), wide)
    put(small_ref, (LANES, LANES), lambda i, j: down_taps(i - 2 * j))
    put(near_ref, (LANES, half), up_pair(near_column, 0))
    put(away_ref, (LANES, half), up_pair(away_column, 1))
    put(narrow_ref, (LANES, half), lambda i, j: up_taps(2 * i - level_one_column(lvl, j)))
    put(raise_ref, (LANES, LANES), lambda i, j: up_taps(2 * i - j))
    wait_all(copies)


def put_kernel(half_ref, out_ref, sems, lvl):
    planes = half_ref.shape[1]
    pairs = []
    for tile, at in enumerate((3 * lvl, 1 + lvl)):
        columns = pl.ds(pl.multiple_of(at * LANES, LANES), LANES)
        for q in range(SUB):
            pairs.append((half_ref.at[tile, :, q, :], out_ref.at[pl.ds(q * planes, planes), columns]))
    wait_all(start_all(pairs, sems))


def put_mine_kernel(mine_ref, out_ref, sems):
    put_kernel(mine_ref, out_ref, sems, lax.axis_index("lvl"))


def put_theirs_kernel(theirs_ref, begun_ref, out_ref, sems):
    put_kernel(theirs_ref, out_ref, sems, 1 - lax.axis_index("lvl"))


def pick(place, weight, values):
    even, odd = values(0), values(1)
    for k in range(2, LEVELS, 2):
        even = jnp.where(place >= float(k - 1), values(k), even)
        odd = jnp.where(place >= float(k), values(k + 1), odd)
    return odd + weight * (even - odd)


def split_store(ref, reduced, column, width):
    for pair in range(len(reduced) // 2):
        both = jnp.concatenate(reduced[2 * pair:2 * pair + 2], axis=0)
        high = both.astype(jnp.bfloat16)
        low = (both - high.astype(jnp.float32)).astype(jnp.bfloat16)
        ref[pair, :, column:column + LANES] = high
        ref[pair, :, width + column:width + column + LANES] = low


def scale_odd(planes):
    return [4.0 * x if p % 2 else x for p, x in enumerate(planes)]


def own_kernel(edge_ref, inner_ref, mine_ref, other_ref, down_ref, gauss_ref, last_ref, tone_ref, place_ref,
               weight_ref, table_ref, cell_scr, rest_scr, part_scr):
    lvl = lax.axis_index("lvl")
    planes = edge_ref.shape[0]
    own = 3 * LANES
    half = 2 * LANES
    pairs = LEVELS // 2

    first = jnp.where(lvl == 0, mine_ref[...], other_ref[...])
    second = jnp.where(lvl == 0, other_ref[...], mine_ref[...])
    for k in range(LEVELS):
        source = first if k < pairs else second
        row = k % pairs
        for kind, table in enumerate(curve_tables(source[row:row + 1, :], k)):
            table_ref[k, kind] = table
    tones = tone_tables(first, second)

    def image(tile, p):
        return edge_ref[p] if tile == 0 else inner_ref[lvl if tile == 1 else 1 - lvl, p]

    for tile in range(3):
        for p in range(planes):
            x = image(tile, p)
            cell_scr[tile, p], rest_scr[tile, p] = curve_cell(p, x)
            if tile < 2:
                tone_ref[tile, p] = tone(tones, x)
                place_ref[tile, p], weight_ref[tile, p] = scaled_level(x)

    def multiply(slot, target):
        part = part_scr[slot].reshape(-1, 2 * own)
        result = dot(part, down_ref[...]).reshape(2, planes // 4, 2, SUB, half)
        for copy in range(2):
            for tile in range(2):
                span = slice(tile * LANES, (tile + 1) * LANES)
                gauss_ref[tile, :, target + copy] = result[copy, :, :, :, span]

    for tile in range(3):
        reduced = rows_down(scale_odd([image(tile, p) for p in range(planes)]), scaled=True)
        for copy in range(2):
            split_store(part_scr.at[1, copy], reduced, tile * LANES, own)

    for step in range(pairs):
        slot = step % 2
        multiply(1 - slot, 2 * step)
        ref = last_ref if step == pairs - 1 else part_scr.at[slot]
        for tile in range(3):
            mapped = remap_pair(
                table_ref, 2 * step, planes, lambda p: cell_scr[tile, p], lambda p: rest_scr[tile, p]
            )
            for copy in range(2):
                split_store(ref.at[copy], rows_down(mapped[copy], scaled=True), tile * LANES, own)


def rest_kernel(halo_ref, gauss_in_ref, last_ref, tone_ref, place_ref, weight_ref, table_ref, down_ref,
                rim_ref, wide_ref, small_ref, near_ref, away_ref, narrow_ref, raise_ref, out_ref, gauss_ref,
                cell_scr, rest_scr, part_scr, up_scr):
    planes = halo_ref.shape[0]
    half = 2 * LANES
    pairs = LEVELS // 2

    result = dot(last_ref[...].reshape(-1, 6 * LANES), down_ref[...]).reshape(2, planes // 4, 2, SUB, half)
    for copy in range(2):
        gauss_ref[0, :, LEVELS + copy] = result[copy, :, :, :, 0:LANES]
        gauss_ref[1, :, LEVELS + copy] = result[copy, :, :, :, LANES:half]

    def columns_up(tile):
        source = jnp.concatenate([gauss_ref[tile, p // 2, FIRST:, p % 2] for p in range(planes // 2)], axis=0)
        result = dot(halves(source.reshape(-1, LANES)), tables_up[tile][...])
        up_scr[tile] = result.reshape(planes // 2, LEVELS, SUB, half)

    tables_up = (near_ref, away_ref)
    for p in range(planes):
        cell_scr[p], rest_scr[p] = curve_cell(p, halo_ref[p])

    def multiply(slot, target):
        part = part_scr[slot].reshape(-1, 2 * RIM)
        result = dot(part, rim_ref[...]).reshape(2, planes // 4, 2, SUB, LANES)
        before = gauss_ref if target == LEVELS else gauss_in_ref
        for copy in range(2):
            gauss_ref[0, :, target + copy] = before[0, :, target + copy] + result[copy]

    reduced = rows_down(scale_odd([halo_ref[p] for p in range(planes)]), scaled=True)
    for copy in range(2):
        split_store(part_scr.at[1, copy], reduced, 0, RIM)
    for step in range(pairs):
        slot = step % 2
        multiply(1 - slot, 2 * step)
        mapped = remap_pair(table_ref, 2 * step, planes, lambda p: cell_scr[p], lambda p: rest_scr[p])
        for copy in range(2):
            split_store(part_scr.at[slot, copy], rows_down(mapped[copy], scaled=True), 0, RIM)
    multiply((pairs - 1) % 2, 2 * pairs)

    sums = {}

    def quarter_sum(tile, at):
        if (tile, at) not in sums:
            count = planes // 2
            edge = lambda p: up_scr[tile, p, :, :, LANES:half]
            if at == 0:
                before = jnp.where(sublane(edge(0)) == 0, edge(0), shift_down(edge(count - 1)))
            else:
                before = edge(at - 1)
            if at == count:
                after = jnp.where(sublane(edge(0)) == SUB - 1, edge(count - 1), shift_up(edge(0)))
            else:
                after = edge(at)
            sums[tile, at] = before + after
        return sums[tile, at]

    def level_zero(tile, p):
        above, below = quarter_sum(tile, p // 2), quarter_sum(tile, p // 2 + 1)
        at = (place_ref[tile, p], weight_ref[tile, p])
        if p % 2 == 0:
            detail = pick(*at, lambda k: (above[k] + below[k]) + up_scr[tile, p // 2, k, :, 0:LANES])
        else:
            detail = 4.0 * pick(*at, lambda k: below[k])
        out_ref[tile, p] = tone_ref[tile, p] - detail

    waiting = [(tile, p) for tile in (1, 0) for p in range(planes)]

    def meanwhile(count):
        for _ in range(min(count, len(waiting))):
            level_zero(*waiting.pop(0))

    def level_one(p):
        return jnp.concatenate([gauss_ref[tile, p // 2, :, p % 2] for tile in range(2)], axis=-1)

    def next_level(coarse, table):
        reduced = rows_down(coarse)
        stacked = jnp.concatenate(reduced, axis=0)
        result = dot(halves(stacked.reshape(-1, stacked.shape[-1])), table)
        result = result.reshape(len(reduced), STACK, SUB, LANES)
        return [result[p] for p in range(len(reduced))]

    def raise_columns(stacks, table):
        stacked = jnp.concatenate(stacks, axis=0)
        result = dot(halves(stacked.reshape(-1, LANES)), table)
        return result.reshape((len(stacks), -1, SUB, table.shape[1]))

    def raise_stack(coarse, table):
        result = raise_columns([plane[FIRST:] for plane in coarse], table)
        return rows_up([result[p] for p in range(len(coarse))])

    def raise_one(planes_of, table):
        result = raise_columns([plane[None] for plane in planes_of], table)
        return rows_up([result[p, 0] for p in range(len(planes_of))])

    def coefficient(level, raised, p):
        here = gauss[level][p]
        return pick(*scaled_level(here[0]), lambda k: here[FIRST + k] - raised[p][k])

    lift = raise_ref[...]
    gauss = [None, [level_one(p) for p in range(planes // 2)]]
    gauss.append(next_level(gauss[1], wide_ref[...]))
    raised = [None, raise_stack(gauss[2], narrow_ref[...])]
    columns_up(1)
    columns_up(0)
    coeffs = [None, []]
    quarter = planes // 8
    for level in range(2, PYR - 1):
        gauss.append(next_level(gauss[level], small_ref[...]))
        coeffs[1] += [coefficient(1, raised[1], p) for p in range(quarter * (level - 2), quarter * (level - 1))]
        raised.append(raise_stack(gauss[level + 1], lift))
    base = raise_one([gauss[PYR - 1][0][0]], lift)
    coeffs[1] += [coefficient(1, raised[1], p) for p in range(3 * quarter, planes // 2)]
    for level in range(2, PYR - 1):
        coeffs.append([coefficient(level, raised[level], p) for p in range(len(gauss[level]))])
    for level in range(PYR - 2, 0, -1):
        out = [one + two for one, two in zip(coeffs[level], base)]
        if level > 1:
            base = raise_one(out, narrow_ref[...] if level == 2 else lift)
        else:
            base = []
            for tile in range(2):
                span = slice(tile * LANES, (tile + 1) * LANES)
                base.append(raise_one([plane[:, span] for plane in out], tables_up[tile][:, 0:LANES]))
        meanwhile(planes // 2)
    meanwhile(2 * planes)
    for tile in range(2):
        for p in range(planes):
            out_ref[tile, p] = out_ref[tile, p] + base[tile][p]


def call(kernel, name, in_specs, out_shape, scratch, out_space=VMEM, **others):
    return pl.pallas_call(
        kernel,
        name=name,
        in_specs=in_specs,
        out_specs=jax.tree.map(lambda _: out_space, out_shape),
        out_shape=out_shape,
        scratch_shapes=scratch,
        compiler_params=PARAMS,
        **others,
    )


def body(image, curves):
    rows, width = image.shape
    planes = rows // SUB
    half = width // 2
    count = lax.axis_size("tile")
    f32 = lambda *shape: jax.ShapeDtypeStruct(shape, jnp.float32)
    b16 = lambda *shape: jax.ShapeDtypeStruct(shape, jnp.bfloat16)
    fast = lambda *shape: pltpu.VMEM(shape, jnp.float32)
    fast_int = lambda *shape: pltpu.VMEM(shape, jnp.int32)
    fast_half = lambda *shape: pltpu.VMEM(shape, jnp.bfloat16)
    in_hbm = lambda x: pltpu.with_memory_space_constraint(x, pltpu.HBM)
    swap = [(0, 1), (1, 0)]

    other_curves = lax.ppermute(curves, "lvl", swap)
    edge, inner, mine, down, rim, wide, small, near, away, narrow, lift = call(
        stage_kernel, "stage", [HBM] * 2,
        [f32(planes, SUB, LANES), f32(2, planes, SUB, LANES), f32(*curves.shape), b16(6 * LANES, half),
         b16(2 * RIM, LANES), b16(2 * half, LANES), b16(2 * LANES, LANES), b16(2 * LANES, half),
         b16(2 * LANES, half), b16(2 * LANES, half), b16(2 * LANES, LANES)],
        [pltpu.SemaphoreType.DMA((3 * SUB + 1,))],
    )(in_hbm(image), in_hbm(curves))
    sent, other_curves = lax.optimization_barrier((edge, other_curves))
    pairs = []
    for tile in range(count):
        pairs.append((2 * tile + 1, 2 * ((tile + 1) % count)))
        pairs.append((2 * tile, 2 * ((tile - 1) % count) + 1))
    halo = lax.ppermute(sent, ("tile", "lvl"), pairs)

    gauss_shape = f32(2, planes // 4, STACK, 2, SUB, LANES)
    out_shape = f32(2, planes, SUB, LANES)
    last_shape = b16(2, planes // 4, 2 * SUB, 6 * LANES)
    gauss, last, toned, place, weight, tables = call(
        own_kernel, "own", [VMEM] * 5,
        [gauss_shape, last_shape, out_shape, out_shape, out_shape, f32(LEVELS, TABLES, SUB, LANES)],
        [fast_int(3, planes, SUB, LANES), fast(3, planes, SUB, LANES), fast_half(2, *last_shape.shape)],
    )(sent, inner, mine, other_curves, down)
    mine, _ = call(
        rest_kernel, "rest", [VMEM] * 15, [out_shape, gauss_shape],
        [fast_int(planes, SUB, RIM), fast(planes, SUB, RIM),
         fast_half(2, 2, planes // 4, 2 * SUB, 2 * RIM), fast(2, planes // 2, LEVELS, SUB, half)],
        input_output_aliases={1: 1},
    )(halo, gauss, last, toned, place, weight, tables, down, rim, wide, small, near, away, narrow, lift)
    theirs = lax.ppermute(mine, "lvl", swap)
    sems = [pltpu.SemaphoreType.DMA((2 * SUB,))]
    begun = call(put_mine_kernel, "put_mine", [VMEM], f32(rows, width), sems, HBM)(mine)
    return call(
        put_theirs_kernel, "put_theirs", [VMEM, HBM], f32(rows, width), sems, HBM, input_output_aliases={1: 0}
    )(theirs, begun)


def solution(mesh):
    placed = (P("band", "tile"), P("lvl", None))
    return jax.shard_map(
        body, mesh=mesh, in_specs=placed, out_specs=P("band", "tile"), check_vma=False
    )
```

time: 17.7 us -> 17.3 us (0.977)
  Pallas kernels: 10.5 us -> 10.1 us
    pallas_call x3, Pallas kernels: 9.06 us -> 8.49 us  [the longest x1 4.16 us: body(): call(rest_kernel, 'rest', [VMEM] * 15, [out_shape, gauss_shape], [fast_in...]
  transfers between devices with their start and end apart: 3 -> 3, of which waited for: 1 -> 1; matrix products, arithmetic and copies ran while one was open for 0% -> 0% of each run, Pallas kernels for 32% -> 30%
where the time goes in v3:
time: 17.3 us; the launch traced here: 17.1 us
  Pallas kernels  10.1 us (58%)
  starting transfers between devices  6.26 us (36%)
  waiting for transfers between devices  0.68 us (4%)
    ppermute x1, starting transfers between devices, body(): halo = lax.ppermute(sent, ('tile', 'lvl'), pairs)  5.73 us
    pallas_call x1, Pallas kernels, body(): call(rest_kernel, 'rest', [VMEM] * 15, [out_shape, gauss_shape], [fast_in...  4.16 us
    pallas_call x1, Pallas kernels, body(): call(own_kernel, 'own', [VMEM] * 5, [gauss_shape, last_shape, out_shape,...  3.14 us
    pallas_call x1, Pallas kernels, body(): call(stage_kernel, 'stage', [HBM] * 2, [f32(planes, SUB, LANES), f32(2, p...  1.2 us
    pallas_call x1, Pallas kernels, body(): call(put_mine_kernel, 'put_mine', [VMEM], f32(rows, width), sems, HBM)(mine)  0.84 us
    pallas_call x1, Pallas kernels, body(): call(put_theirs_kernel, 'put_theirs', [VMEM, HBM], f32(rows, width), sems...  0.83 us
    ppermute x1, waiting for transfers between devices, body(): theirs = lax.ppermute(mine, 'lvl', swap)  0.68 us
    ppermute x1, starting transfers between devices, body(): other_curves = lax.ppermute(curves, 'lvl', swap)  0.45 us
  transfers between devices with their start and end apart: 3, of which 1 were waited for; matrix products, arithmetic and copies ran while one was open for 0% of the time, Pallas kernels for 30%

profile of v3, /device:TPU:0, one launch (start us, length us, event | category | flops | bytes accessed | tf_op | source)
XLA Modules:
  0.0 17.1 jit_solution(4670018618980231618)
XLA Ops:
  0.0 0.5 %collective-permute-start = (f32[8,17]{1,0:T(8,128)}, f32[8,17]{1,0:T(8,128)S(1)}, u32[]{:S(2)}, u32[]{:S(2)}) collective-permute-start(f32[8,17]{1,0:T(8,128)} %curves_ref.1), channel_id=1, source_target_pairs={{0,1},{1,0},{2,3},{3,2},{4,5},{5,4},{6,7},{7,6},{8,9},{9,8},{10,11... | collective-permute-start | bytes 1640 | tf_op jit(solution)/shard_map/ppermute | solution.py:548
  0.5 1.2 %stage.1 = (f32[32,8,128]{2,1,0:T(8,128)S(1)}, f32[2,32,8,128]{3,2,1,0:T(8,128)S(1)}, f32[8,17]{1,0:T(8,128)S(1)}, bf16[768,256]{1,0:T(8,128)(2,1)S(1)}, bf16[25...) custom-call(f32[256,512]{1,0:T(8,128)} %image_ref.1, ...), custom_call_target="tpu_custom_call" | custom-call | tf_op jit(solution)/shard_map/stage/pallas_call | solution.py:549
  1.7 0.0 collective-permute-done.other_ref
  1.7 5.7 %collective-permute-start.1 = (f32[32,8,128]{2,1,0:T(8,128)S(1)}, f32[32,8,128]{2,1,0:T(8,128)S(1)}, u32[]{:S(2)}, u32[]{:S(2)}) collective-permute-start(f32[32,8,128]{2,1,0:T(8,128)S(1)} %get-tuple-element.26.edge_ref), channel_id=1, source_target_pairs={{1,2},{0,15},{3,4},{2,1},{5,6},{4,3},{7,8},{6,5},{9,10},{8,7},{11,... | collective-permute-start | bytes 393224 | tf_op jit(solution)/shard_map/ppermute | solution.py:561
  7.4 3.1 %own.1 = (f32[2,8,18,2,8,128]{5,4,3,2,1,0:T(8,128)S(1)}, bf16[2,8,16,768]{3,2,1,0:T(8,128)(2,1)S(1)}, f32[2,32,8,128]{3,2,1,0:T(8,128)S(1)}, f32[2,32,8,128]{3,2...) custom-call(f32[32,8,128]{2,1,0:T(8,128)S(1)} %get-tuple-element.26.edge_ref, ...), custom_call_target="tpu_custom_call" | custom-call | tf_op jit(solution)/shard_map/own/pallas_call | solution.py:566
  10.5 0.0 collective-permute-done.1.halo_ref
  10.6 4.2 %rest.1 = (f32[2,32,8,128]{3,2,1,0:T(8,128)S(1)}, f32[2,8,18,2,8,128]{5,4,3,2,1,0:T(8,128)S(1)}) custom-call(f32[32,8,128]{2,1,0:T(8,128)S(1)} %collective-permute-done.1.halo_ref, f32[2,8,18,2,8,128]{5,4,3,2,1,0:T(8,128)S(1)} %get-tuple-element.31.gauss_in_ref, ...), custom_call_target="tpu_custom_call", output_to_operand_aliasing={{1}: (1, {})} | custom-call | tf_op jit(solution)/shard_map/rest/pallas_call | solution.py:571
  14.7 0.1 collective-permute-start.2
  14.8 0.8 %put_mine.1.begun_ref = f32[256,512]{1,0:T(8,128)} custom-call(f32[2,32,8,128]{3,2,1,0:T(8,128)S(1)} %get-tuple-element.44.mine_ref), custom_call_target="tpu_custom_call" | custom-call | tf_op jit(solution)/shard_map/put_mine/pallas_call | solution.py:579
  15.6 0.7 %collective-permute-done.2.theirs_ref = f32[2,32,8,128]{3,2,1,0:T(8,128)S(1)} collective-permute-done((f32[2,32,8,128]{3,2,1,0:T(8,128)S(1)}, f32[2,32,8,128]{3,2,1,0:T(8,128)S(1)}, u32[]{:S(2)}, u32[]{:S(2)}) %collective-permute-start.2) | collective-permute-done | bytes 262176 | tf_op jit(solution)/shard_map/ppermute | solution.py:577
  16.3 0.8 %put_theirs.1 = f32[256,512]{1,0:T(8,128)} custom-call(f32[2,32,8,128]{3,2,1,0:T(8,128)S(1)} %collective-permute-done.2.theirs_ref, f32[256,512]{1,0:T(8,128)} %put_mine.1.begun_ref), custom_call_target="tpu_custom_call", output_to_operand_aliasing={{}: (1, {})} | custom-call | tf_op jit(solution)/shard_map/put_theirs/pallas_call | solution.py:580
Async XLA Ops:
  0.0 1.7 %collective-permute-start = (f32[8,17]{1,0:T(8,128)}, f32[8,17]{1,0:T(8,128)S(1)}, u32[]{:S(2)}, u32[]{:S(2)}) collective-permute-start(f32[8,17]{1,0:T(8,128)} %curves_ref.1), channel_id=1, source_target_pairs={{0,1},{1,0},{2,3},{3,2},{4,5},{5,4},{6,7},{7,6},{8,9},{9,8},{10,11... | collective-permute-start | bytes 1640 | tf_op jit(solution)/shard_map/ppermute | solution.py:548
  1.7 8.9 %collective-permute-start.1 = (f32[32,8,128]{2,1,0:T(8,128)S(1)}, f32[32,8,128]{2,1,0:T(8,128)S(1)}, u32[]{:S(2)}, u32[]{:S(2)}) collective-permute-start(f32[32,8,128]{2,1,0:T(8,128)S(1)} %get-tuple-element.26.edge_ref), channel_id=1, source_target_pairs={{1,2},{0,15},{3,4},{2,1},{5,6},{4,3},{7,8},{6,5},{9,10},{8,7},{11,... | collective-permute-start | bytes 393224 | tf_op jit(solution)/shard_map/ppermute | solution.py:561
  14.7 1.6 %collective-permute-start.2 = (f32[2,32,8,128]{3,2,1,0:T(8,128)S(1)}, f32[2,32,8,128]{3,2,1,0:T(8,128)S(1)}, u32[]{:S(2)}, u32[]{:S(2)}) collective-permute-start(f32[2,32,8,128]{3,2,1,0:T(8,128)S(1)} %get-tuple-element.44.mine_ref), channel_id=1, source_target_pairs={{0,1},{1,0},{2,3},{3,2},{4,5},{5,4},{6,7},{7,6},{8,9},{9,8},{10,11... | collective-permute-start | bytes 786440 | tf_op jit(solution)/shard_map/ppermute | solution.py:577

commit v4 on v3

--- a/solution.py
+++ b/solution.py
@@ -13,6 +13,7 @@
 
 SUB = 8
 LANES = 128
+PIECE = LANES // 4
 RIM = LANES
 FIRST = 2
 STACK = FIRST + LEVELS
@@ -127,8 +128,8 @@
 
 def curve_tables(curve_row, k):
     steps = (KNOTS - 1) // 2
-    turn = steps * k // (LEVELS - 1)
-    phase = (steps * k % (LEVELS - 1)) / (LEVELS - 1)
+    turn = lax.div(steps * k, LEVELS - 1)
+    phase = (steps * k - (LEVELS - 1) * turn).astype(jnp.float32) / (LEVELS - 1)
     width = curve_row.shape[-1]
     row = jnp.broadcast_to(curve_row, (SUB, width))
     offset = iota((SUB, width), 1) - iota((SUB, width), 0)
@@ -140,10 +141,10 @@
     left, middle, right = node(-1), node(0), node(1)
     slope = middle - left
     bend = (right - middle) - slope
-    start = (k / (LEVELS - 1) + middle) - phase * slope - phase * bend
+    start = (k.astype(jnp.float32) / (LEVELS - 1) + middle) - phase * slope - phase * bend
     spread = lambda v: jnp.broadcast_to(v, (SUB, LANES))
     coarse = (spread(start), spread(slope), spread(bend))
-    phase = jnp.full((SUB, LANES), phase, jnp.float32)
+    phase = spread(phase)
 
     lane = iota((SUB, LANES), 1)
     index = jnp.minimum(jnp.floor((lane.astype(jnp.float32) + 0.5) / (LEVELS - 1)), float(SUB - 1))
@@ -231,6 +232,22 @@
         copy.wait()
 
 
+def kept_lanes(lvl):
+    lane = iota((SUB, LANES), 1)
+    return (lane >= PIECE * lvl) & (lane < LANES - PIECE * (1 - lvl))
+
+
+def unpack(sent, lvl):
+    lane = iota((SUB, LANES), 1)
+    planes = []
+    for group in range(len(sent) // 3):
+        three = sent[3 * group:3 * group + 3]
+        one, two, three_on = [pltpu.roll(x, PIECE * (at + 1), axis=1) for at, x in enumerate(three)]
+        later = jnp.where(lane < PIECE * (2 + lvl), two, three_on)
+        planes += three + [jnp.where(lane < PIECE * (1 + lvl), one, later)]
+    return planes
+
+
 def near_column(lvl, lane):
     return lane + jnp.where(lvl == 0, LEFT, RIGHT)
 
@@ -243,7 +260,7 @@
     return jnp.where(at < LANES, near_column(lvl, at), away_column(lvl, at - LANES))
 
 
-def stage_kernel(image_ref, curves_ref, edge_ref, inner_ref, mine_ref, own_ref, rim_ref, wide_ref,
+def stage_kernel(image_ref, curves_ref, edge_ref, inner_ref, sent_ref, mine_ref, own_ref, rim_ref, wide_ref,
                  small_ref, near_ref, away_ref, narrow_ref, raise_ref, sems):
     lvl = lax.axis_index("lvl")
     planes = edge_ref.shape[0]
@@ -295,6 +312,11 @@
     put(narrow_ref, (LANES, half), lambda i, j: up_taps(2 * i - level_one_column(lvl, j)))
     put(raise_ref, (LANES, LANES), lambda i, j: up_taps(2 * i - j))
     wait_all(copies)
+    kept = kept_lanes(lvl)
+    for group in range(planes // 4):
+        *three, fourth = [edge_ref[4 * group + at] for at in range(4)]
+        for at, x in enumerate(three):
+            sent_ref[3 * group + at] = jnp.where(kept, x, pltpu.roll(fourth, LANES - PIECE * (at + 1), axis=1))
 
 
 def put_kernel(half_ref, out_ref, sems, lvl):
@@ -336,70 +358,102 @@
     return [4.0 * x if p % 2 else x for p, x in enumerate(planes)]
 
 
-def own_kernel(edge_ref, inner_ref, mine_ref, other_ref, down_ref, gauss_ref, last_ref, tone_ref, place_ref,
-               weight_ref, table_ref, cell_scr, rest_scr, part_scr):
+def all_tables(table_ref, curves_ref, first):
+    for row in range(LEVELS // 2):
+        for kind, table in enumerate(curve_tables(curves_ref[row:row + 1, :], first + row)):
+            table_ref[first + row, kind] = table
+
+
+def image_of(edge_ref, inner_ref, tile, p):
     lvl = lax.axis_index("lvl")
+    return edge_ref[p] if tile == 0 else inner_ref[lvl if tile == 1 else 1 - lvl, p]
+
+
+def multiply_own(part_ref, down_ref, gauss_ref, target):
+    part = part_ref[...].reshape(-1, 6 * LANES)
+    result = dot(part, down_ref[...]).reshape(2, part_ref.shape[1], 2, SUB, 2 * LANES)
+    for copy in range(2):
+        for tile in range(2):
+            span = slice(tile * LANES, (tile + 1) * LANES)
+            gauss_ref[tile, :, target + copy] = result[copy, :, :, :, span]
+
+
+def own_pairs(table_ref, first, cell_ref, fraction_ref, down_ref, gauss_ref, last_ref, part_scr, before):
+    planes = cell_ref.shape[1]
+    pairs = LEVELS // 4
+    waiting = before
+    for step in range(pairs):
+        multiply_own(waiting[0], down_ref, gauss_ref, waiting[1])
+        ref = last_ref if step == pairs - 1 else part_scr.at[step % 2]
+        for tile in range(3):
+            mapped = remap_pair(
+                table_ref, first + 2 * step, planes, lambda p: cell_ref[tile, p], lambda p: fraction_ref[tile, p]
+            )
+            for copy in range(2):
+                split_store(ref.at[copy], rows_down(mapped[copy], scaled=True), tile * LANES, 3 * LANES)
+        waiting = (ref, FIRST + first + 2 * step)
+
+
+def waits_longest():
+    return (lax.axis_index("band") == 0) & (lax.axis_index("tile") == 0) & (lax.axis_index("lvl") == 0)
+
+
+def early_kernel(*refs):
+    @pl.when(waits_longest())
+    def _():
+        mine_part(*refs)
+
+
+def late_kernel(*refs):
+    @pl.when(jnp.logical_not(waits_longest()))
+    def _():
+        mine_part(*refs[:4], *refs[11:])
+
+
+def mine_part(edge_ref, inner_ref, mine_ref, down_ref, gauss_ref, last_ref, place_ref, weight_ref,
+                table_ref, cell_ref, fraction_ref, part_scr):
     planes = edge_ref.shape[0]
-    own = 3 * LANES
-    half = 2 * LANES
-    pairs = LEVELS // 2
-
-    first = jnp.where(lvl == 0, mine_ref[...], other_ref[...])
-    second = jnp.where(lvl == 0, other_ref[...], mine_ref[...])
-    for k in range(LEVELS):
-        source = first if k < pairs else second
-        row = k % pairs
-        for kind, table in enumerate(curve_tables(source[row:row + 1, :], k)):
-            table_ref[k, kind] = table
-    tones = tone_tables(first, second)
-
-    def image(tile, p):
-        return edge_ref[p] if tile == 0 else inner_ref[lvl if tile == 1 else 1 - lvl, p]
-
+    first = lax.axis_index("lvl") * (LEVELS // 2)
+    all_tables(table_ref, mine_ref, first)
+    image = functools.partial(image_of, edge_ref, inner_ref)
     for tile in range(3):
         for p in range(planes):
             x = image(tile, p)
-            cell_scr[tile, p], rest_scr[tile, p] = curve_cell(p, x)
+            cell_ref[tile, p], fraction_ref[tile, p] = curve_cell(p, x)
             if tile < 2:
-                tone_ref[tile, p] = tone(tones, x)
                 place_ref[tile, p], weight_ref[tile, p] = scaled_level(x)
-
-    def multiply(slot, target):
-        part = part_scr[slot].reshape(-1, 2 * own)
-        result = dot(part, down_ref[...]).reshape(2, planes // 4, 2, SUB, half)
-        for copy in range(2):
-            for tile in range(2):
-                span = slice(tile * LANES, (tile + 1) * LANES)
-                gauss_ref[tile, :, target + copy] = result[copy, :, :, :, span]
-
-    for tile in range(3):
         reduced = rows_down(scale_odd([image(tile, p) for p in range(planes)]), scaled=True)
         for copy in range(2):
-            split_store(part_scr.at[1, copy], reduced, tile * LANES, own)
-
-    for step in range(pairs):
-        slot = step % 2
-        multiply(1 - slot, 2 * step)
-        ref = last_ref if step == pairs - 1 else part_scr.at[slot]
-        for tile in range(3):
-            mapped = remap_pair(
-                table_ref, 2 * step, planes, lambda p: cell_scr[tile, p], lambda p: rest_scr[tile, p]
-            )
-            for copy in range(2):
-                split_store(ref.at[copy], rows_down(mapped[copy], scaled=True), tile * LANES, own)
+            split_store(part_scr.at[1, copy], reduced, tile * LANES, 3 * LANES)
+    before = (part_scr.at[1], 0)
+    own_pairs(table_ref, first, cell_ref, fraction_ref, down_ref, gauss_ref, last_ref, part_scr, before)
+
+
+def other_kernel(edge_ref, inner_ref, mine_ref, other_ref, down_ref, cell_ref, fraction_ref, last_in_ref,
+                 gauss_in_ref, table_in_ref, gauss_ref, table_ref, last_ref, tone_ref, part_scr):
+    lvl = lax.axis_index("lvl")
+    first = (1 - lvl) * (LEVELS // 2)
+    all_tables(table_ref, other_ref, first)
+    low = jnp.where(lvl == 0, mine_ref[...], other_ref[...])
+    high = jnp.where(lvl == 0, other_ref[...], mine_ref[...])
+    tones = tone_tables(low, high)
+    for tile in range(2):
+        for p in range(edge_ref.shape[0]):
+            tone_ref[tile, p] = tone(tones, image_of(edge_ref, inner_ref, tile, p))
+    before = (last_in_ref, FIRST + lvl * (LEVELS // 2) + LEVELS // 2 - 2)
+    own_pairs(table_ref, first, cell_ref, fraction_ref, down_ref, gauss_ref, last_ref, part_scr, before)
 
 
 def rest_kernel(halo_ref, gauss_in_ref, last_ref, tone_ref, place_ref, weight_ref, table_ref, down_ref,
                 rim_ref, wide_ref, small_ref, near_ref, away_ref, narrow_ref, raise_ref, out_ref, gauss_ref,
                 cell_scr, rest_scr, part_scr, up_scr):
-    planes = halo_ref.shape[0]
+    lvl = lax.axis_index("lvl")
+    halo = unpack([halo_ref[at] for at in range(halo_ref.shape[0])], 1 - lvl)
+    planes = len(halo)
     half = 2 * LANES
     pairs = LEVELS // 2
 
-    result = dot(last_ref[...].reshape(-1, 6 * LANES), down_ref[...]).reshape(2, planes // 4, 2, SUB, half)
-    for copy in range(2):
-        gauss_ref[0, :, LEVELS + copy] = result[copy, :, :, :, 0:LANES]
-        gauss_ref[1, :, LEVELS + copy] = result[copy, :, :, :, LANES:half]
+    multiply_own(last_ref, down_ref, gauss_ref, FIRST + (1 - lvl) * (LEVELS // 2) + LEVELS // 2 - 2)
 
     def columns_up(tile):
         source = jnp.concatenate([gauss_ref[tile, p // 2, FIRST:, p % 2] for p in range(planes // 2)], axis=0)
@@ -408,16 +462,15 @@
 
     tables_up = (near_ref, away_ref)
     for p in range(planes):
-        cell_scr[p], rest_scr[p] = curve_cell(p, halo_ref[p])
+        cell_scr[p], rest_scr[p] = curve_cell(p, halo[p])
 
     def multiply(slot, target):
         part = part_scr[slot].reshape(-1, 2 * RIM)
         result = dot(part, rim_ref[...]).reshape(2, planes // 4, 2, SUB, LANES)
-        before = gauss_ref if target == LEVELS else gauss_in_ref
         for copy in range(2):
-            gauss_ref[0, :, target + copy] = before[0, :, target + copy] + result[copy]
-
-    reduced = rows_down(scale_odd([halo_ref[p] for p in range(planes)]), scaled=True)
+            gauss_ref[0, :, target + copy] = gauss_ref[0, :, target + copy] + result[copy]
+
+    reduced = rows_down(scale_odd(halo), scaled=True)
     for copy in range(2):
         split_store(part_scr.at[1, copy], reduced, 0, RIM)
     for step in range(pairs):
@@ -540,34 +593,44 @@
     f32 = lambda *shape: jax.ShapeDtypeStruct(shape, jnp.float32)
     b16 = lambda *shape: jax.ShapeDtypeStruct(shape, jnp.bfloat16)
     fast = lambda *shape: pltpu.VMEM(shape, jnp.float32)
+    i32 = lambda *shape: jax.ShapeDtypeStruct(shape, jnp.int32)
     fast_int = lambda *shape: pltpu.VMEM(shape, jnp.int32)
     fast_half = lambda *shape: pltpu.VMEM(shape, jnp.bfloat16)
     in_hbm = lambda x: pltpu.with_memory_space_constraint(x, pltpu.HBM)
     swap = [(0, 1), (1, 0)]
 
-    other_curves = lax.ppermute(curves, "lvl", swap)
-    edge, inner, mine, down, rim, wide, small, near, away, narrow, lift = call(
+    edge, inner, sent, mine, down, rim, wide, small, near, away, narrow, lift = call(
         stage_kernel, "stage", [HBM] * 2,
-        [f32(planes, SUB, LANES), f32(2, planes, SUB, LANES), f32(*curves.shape), b16(6 * LANES, half),
+        [f32(planes, SUB, LANES), f32(2, planes, SUB, LANES), f32(planes * 3 // 4, SUB, LANES), f32(*curves.shape), b16(6 * LANES, half),
          b16(2 * RIM, LANES), b16(2 * half, LANES), b16(2 * LANES, LANES), b16(2 * LANES, half),
          b16(2 * LANES, half), b16(2 * LANES, half), b16(2 * LANES, LANES)],
         [pltpu.SemaphoreType.DMA((3 * SUB + 1,))],
     )(in_hbm(image), in_hbm(curves))
-    sent, other_curves = lax.optimization_barrier((edge, other_curves))
     pairs = []
     for tile in range(count):
         pairs.append((2 * tile + 1, 2 * ((tile + 1) % count)))
         pairs.append((2 * tile, 2 * ((tile - 1) % count) + 1))
-    halo = lax.ppermute(sent, ("tile", "lvl"), pairs)
 
     gauss_shape = f32(2, planes // 4, STACK, 2, SUB, LANES)
     out_shape = f32(2, planes, SUB, LANES)
     last_shape = b16(2, planes // 4, 2 * SUB, 6 * LANES)
-    gauss, last, toned, place, weight, tables = call(
-        own_kernel, "own", [VMEM] * 5,
-        [gauss_shape, last_shape, out_shape, out_shape, out_shape, f32(LEVELS, TABLES, SUB, LANES)],
-        [fast_int(3, planes, SUB, LANES), fast(3, planes, SUB, LANES), fast_half(2, *last_shape.shape)],
-    )(sent, inner, mine, other_curves, down)
+    table_shape = f32(LEVELS, TABLES, SUB, LANES)
+    strip = (3, planes, SUB, LANES)
+    part = [fast_half(2, *last_shape.shape)]
+    own_shapes = [gauss_shape, last_shape, out_shape, out_shape, table_shape, i32(*strip), f32(*strip)]
+    begun = call(early_kernel, "early", [VMEM] * 4, own_shapes, part)(edge, inner, mine, down)
+    sent, begun = lax.optimization_barrier((sent, begun))
+    halo = lax.ppermute(sent, ("tile", "lvl"), pairs)
+    gauss, last, place, weight, tables, cells, fractions = call(
+        late_kernel, "late", [VMEM] * 11, own_shapes, part,
+        input_output_aliases={4 + at: at for at in range(7)},
+    )(edge, inner, mine, down, *begun)
+    swapped, last = lax.optimization_barrier((mine, last))
+    other_curves = lax.ppermute(swapped, "lvl", swap)
+    gauss, tables, last, toned = call(
+        other_kernel, "other", [VMEM] * 10, [gauss_shape, table_shape, last_shape, out_shape], part,
+        input_output_aliases={8: 0, 9: 1},
+    )(edge, inner, mine, other_curves, down, cells, fractions, last, gauss, tables)
     mine, _ = call(
         rest_kernel, "rest", [VMEM] * 15, [out_shape, gauss_shape],
         [fast_int(planes, SUB, RIM), fast(planes, SUB, RIM),

time: 17.3 us -> 17.1 us (0.988)
  the two profiles are of different devices: /device:TPU:0 before, /device:TPU:3 now
where the time goes in v4:
time: 17.1 us; the launch traced here: 16.9 us
  Pallas kernels  10.5 us (61%)
  starting transfers between devices  5.21 us (30%)
  waiting for transfers between devices  1.18 us (7%)
    pallas_call x1, Pallas kernels, body(): call(rest_kernel, 'rest', [VMEM] * 15, [out_shape, gauss_shape], [fast_in...  4.12 us
    ppermute x1, starting transfers between devices, body(): other_curves = lax.ppermute(swapped, 'lvl', swap)  2.94 us
    ppermute x1, starting transfers between devices, body(): halo = lax.ppermute(sent, ('tile', 'lvl'), pairs)  1.87 us
    pallas_call x1, Pallas kernels, body(): call(late_kernel, 'late', [VMEM] * 11, own_shapes, part, input_output_ali...  1.71 us
    pallas_call x1, Pallas kernels, body(): call(other_kernel, 'other', [VMEM] * 10, [gauss_shape, table_shape, last_...  1.67 us
    pallas_call x1, Pallas kernels, body(): call(stage_kernel, 'stage', [HBM] * 2, [f32(planes, SUB, LANES), f32(2, p...  1.29 us
    pallas_call x1, Pallas kernels, body(): call(put_theirs_kernel, 'put_theirs', [VMEM, HBM], f32(rows, width), sems...  0.83 us
    pallas_call x1, Pallas kernels, body(): call(put_mine_kernel, 'put_mine', [VMEM], f32(rows, width), sems, HBM)(mine)  0.83 us
  transfers between devices with their start and end apart: 3, of which 2 were waited for; matrix products, arithmetic and copies ran while one was open for 0% of the time, Pallas kernels for 25%

profile of v4, /device:TPU:3, one launch (start us, length us, event | category | flops | bytes accessed | tf_op | source)
XLA Modules:
  0.0 16.9 jit_solution(16475632072185662721)
XLA Ops:
  0.0 1.3 %stage.1 = (f32[32,8,128]{2,1,0:T(8,128)S(1)}, f32[2,32,8,128]{3,2,1,0:T(8,128)S(1)}, f32[24,8,128]{2,1,0:T(8,128)S(1)}, f32[8,17]{1,0:T(8,128)S(1)}, bf16[768,2...) custom-call(f32[256,512]{1,0:T(8,128)} %image_ref.1, ...), custom_call_target="tpu_custom_call" | custom-call | tf_op jit(solution)/shard_map/stage/pallas_call | solution.py:602
  1.3 1.9 %collective-permute-start = (f32[24,8,128]{2,1,0:T(8,128)S(1)}, f32[24,8,128]{2,1,0:T(8,128)S(1)}, u32[]{:S(2)}, u32[]{:S(2)}) collective-permute-start(f32[24,8,128]{2,1,0:T(8,128)S(1)} %get-tuple-element.58), channel_id=1, source_target_pairs={{1,2},{0,15},{3,4},{2,1},{5,6},{4,3},{7,8},{6,5},{9,10},{8,7},{11,... | collective-permute-start | bytes 294920 | tf_op jit(solution)/shard_map/ppermute | solution.py:623
  3.2 1.7 %late.1 = (f32[2,8,18,2,8,128]{5,4,3,2,1,0:T(8,128)S(1)}, bf16[2,8,16,768]{3,2,1,0:T(8,128)(2,1)S(1)}, f32[2,32,8,128]{3,2,1,0:T(8,128)S(1)}, f32[2,32,8,128]{3,...) custom-call(f32[32,8,128]{2,1,0:T(8,128)S(1)} %get-tuple-element.47., ...), custom_call_target="tpu_custom_call", output_to_operand_aliasing={{0}: (4, {}), {1}: (5, {}), {2}: (6, {}), {3}: (7, {}), {4}... | custom-call | tf_op jit(solution)/shard_map/late/pallas_call | solution.py:624
  4.9 2.9 %collective-permute-start.1 = (f32[8,17]{1,0:T(8,128)S(1)}, f32[8,17]{1,0:T(8,128)S(1)}, u32[]{:S(2)}, u32[]{:S(2)}) collective-permute-start(f32[8,17]{1,0:T(8,128)S(1)} %get-tuple-element.67.refs_2_.mine_ref), channel_id=1, source_target_pairs={{0,1},{1,0},{2,3},{3,2},{4,5},{5,4},{6,7},{7,6},{8,9},{9,8},{10,11... | collective-permute-start | bytes 1640 | tf_op jit(solution)/shard_map/ppermute | solution.py:629
  7.8 0.8 %collective-permute-done.1.other_ref = f32[8,17]{1,0:T(8,128)S(1)} collective-permute-done((f32[8,17]{1,0:T(8,128)S(1)}, f32[8,17]{1,0:T(8,128)S(1)}, u32[]{:S(2)}, u32[]{:S(2)}) %collective-permute-start.1) | collective-permute-done | bytes 576 | tf_op jit(solution)/shard_map/ppermute | solution.py:629
  8.7 1.7 %other.1 = (f32[2,8,18,2,8,128]{5,4,3,2,1,0:T(8,128)S(1)}, f32[16,11,8,128]{3,2,1,0:T(8,128)S(1)}, bf16[2,8,16,768]{3,2,1,0:T(8,128)(2,1)S(1)}, f32[2,32,8,128]{3,2,1,0:T(8,128)S(1)}) custom-call(f32[32,8,128]{2,1,0:T(8,128)S(1)} %get-tuple-element.47.refs_0_.edge_ref, ...), custom_call_target="tpu_custom_call", output_to_operand_aliasing={{0}: (8, {}), {1}: (9, {})} | custom-call | tf_op jit(solution)/shard_map/other/pallas_call | solution.py:630
  10.4 0.0 collective-permute-done.halo_ref
  10.4 4.1 %rest.1 = (f32[2,32,8,128]{3,2,1,0:T(8,128)S(1)}, f32[2,8,18,2,8,128]{5,4,3,2,1,0:T(8,128)S(1)}) custom-call(f32[24,8,128]{2,1,0:T(8,128)S(1)} %collective-permute-done.halo_ref, f32[2,8,18,2,8,128]{5,4,3,2,1,0:T(8,128)S(1)} %get-tuple-element.73.gauss_in_ref, ...), custom_call_target="tpu_custom_call", output_to_operand_aliasing={{1}: (1, {})} | custom-call | tf_op jit(solution)/shard_map/rest/pallas_call | solution.py:634
  14.5 0.4 %collective-permute-start.2 = (f32[2,32,8,128]{3,2,1,0:T(8,128)S(1)}, f32[2,32,8,128]{3,2,1,0:T(8,128)S(1)}, u32[]{:S(2)}, u32[]{:S(2)}) collective-permute-start(f32[2,32,8,128]{3,2,1,0:T(8,128)S(1)} %get-tuple-element.86.mine_ref), channel_id=1, source_target_pairs={{0,1},{1,0},{2,3},{3,2},{4,5},{5,4},{6,7},{7,6},{8,9},{9,8},{10,11... | collective-permute-start | bytes 786440 | tf_op jit(solution)/shard_map/ppermute | solution.py:640
  14.9 0.8 %put_mine.1.begun_ref = f32[256,512]{1,0:T(8,128)} custom-call(f32[2,32,8,128]{3,2,1,0:T(8,128)S(1)} %get-tuple-element.86.mine_ref), custom_call_target="tpu_custom_call" | custom-call | tf_op jit(solution)/shard_map/put_mine/pallas_call | solution.py:642
  15.7 0.4 %collective-permute-done.2.theirs_ref = f32[2,32,8,128]{3,2,1,0:T(8,128)S(1)} collective-permute-done((f32[2,32,8,128]{3,2,1,0:T(8,128)S(1)}, f32[2,32,8,128]{3,2,1,0:T(8,128)S(1)}, u32[]{:S(2)}, u32[]{:S(2)}) %collective-permute-start.2) | collective-permute-done | bytes 262176 | tf_op jit(solution)/shard_map/ppermute | solution.py:640
  16.1 0.8 %put_theirs.1 = f32[256,512]{1,0:T(8,128)} custom-call(f32[2,32,8,128]{3,2,1,0:T(8,128)S(1)} %collective-permute-done.2.theirs_ref, f32[256,512]{1,0:T(8,128)} %put_mine.1.begun_ref), custom_call_target="tpu_custom_call", output_to_operand_aliasing={{}: (1, {})} | custom-call | tf_op jit(solution)/shard_map/put_theirs/pallas_call | solution.py:643
  (1 shorter events, 0.0 us)
Async XLA Ops:
  1.3 9.0 %collective-permute-start = (f32[24,8,128]{2,1,0:T(8,128)S(1)}, f32[24,8,128]{2,1,0:T(8,128)S(1)}, u32[]{:S(2)}, u32[]{:S(2)}) collective-permute-start(f32[24,8,128]{2,1,0:T(8,128)S(1)} %get-tuple-element.58), channel_id=1, source_target_pairs={{1,2},{0,15},{3,4},{2,1},{5,6},{4,3},{7,8},{6,5},{9,10},{8,7},{11,... | collective-permute-start | bytes 294920 | tf_op jit(solution)/shard_map/ppermute | solution.py:623
  4.9 3.8 %collective-permute-start.1 = (f32[8,17]{1,0:T(8,128)S(1)}, f32[8,17]{1,0:T(8,128)S(1)}, u32[]{:S(2)}, u32[]{:S(2)}) collective-permute-start(f32[8,17]{1,0:T(8,128)S(1)} %get-tuple-element.67.refs_2_.mine_ref), channel_id=1, source_target_pairs={{0,1},{1,0},{2,3},{3,2},{4,5},{5,4},{6,7},{7,6},{8,9},{9,8},{10,11... | collective-permute-start | bytes 1640 | tf_op jit(solution)/shard_map/ppermute | solution.py:629
  14.5 1.6 %collective-permute-start.2 = (f32[2,32,8,128]{3,2,1,0:T(8,128)S(1)}, f32[2,32,8,128]{3,2,1,0:T(8,128)S(1)}, u32[]{:S(2)}, u32[]{:S(2)}) collective-permute-start(f32[2,32,8,128]{3,2,1,0:T(8,128)S(1)} %get-tuple-element.86.mine_ref), channel_id=1, source_target_pairs={{0,1},{1,0},{2,3},{3,2},{4,5},{5,4},{6,7},{7,6},{8,9},{9,8},{10,11... | collective-permute-start | bytes 786440 | tf_op jit(solution)/shard_map/ppermute | solution.py:640

commit v5 on v4

--- a/solution.py
+++ b/solution.py
@@ -395,7 +395,8 @@
 
 
 def waits_longest():
-    return (lax.axis_index("band") == 0) & (lax.axis_index("tile") == 0) & (lax.axis_index("lvl") == 0)
+    foremost = (lax.axis_index("band") == 0) | (lax.axis_index("lvl") == 1)
+    return (lax.axis_index("tile") == 0) & foremost
 
 
 def early_kernel(*refs):
@@ -619,14 +620,13 @@
     part = [fast_half(2, *last_shape.shape)]
     own_shapes = [gauss_shape, last_shape, out_shape, out_shape, table_shape, i32(*strip), f32(*strip)]
     begun = call(early_kernel, "early", [VMEM] * 4, own_shapes, part)(edge, inner, mine, down)
-    sent, begun = lax.optimization_barrier((sent, begun))
+    sent, mine, begun = lax.optimization_barrier((sent, mine, begun))
     halo = lax.ppermute(sent, ("tile", "lvl"), pairs)
+    other_curves = lax.ppermute(mine, "lvl", swap)
     gauss, last, place, weight, tables, cells, fractions = call(
         late_kernel, "late", [VMEM] * 11, own_shapes, part,
         input_output_aliases={4 + at: at for at in range(7)},
     )(edge, inner, mine, down, *begun)
-    swapped, last = lax.optimization_barrier((mine, last))
-    other_curves = lax.ppermute(swapped, "lvl", swap)
     gauss, tables, last, toned = call(
         other_kernel, "other", [VMEM] * 10, [gauss_shape, table_shape, last_shape, out_shape], part,
         input_output_aliases={8: 0, 9: 1},

time: 17.1 us -> 16.6 us (0.971)
  the two profiles are of different devices: /device:TPU:3 before, /device:TPU:0 now
where the time goes in v5:
time: 16.6 us; the launch traced here: 16.4 us
  Pallas kernels  10.5 us (63%)
  starting transfers between devices  3.86 us (23%)
  waiting for transfers between devices  2.01 us (12%)
    pallas_call x1, Pallas kernels, body(): call(rest_kernel, 'rest', [VMEM] * 15, [out_shape, gauss_shape], [fast_in...  4.12 us
    ppermute x1, starting transfers between devices, body(): halo = lax.ppermute(sent, ('tile', 'lvl'), pairs)  3.79 us
    pallas_call x1, Pallas kernels, body(): call(early_kernel, 'early', [VMEM] * 4, own_shapes, part)  1.75 us
    pallas_call x1, Pallas kernels, body(): call(other_kernel, 'other', [VMEM] * 10, [gauss_shape, table_shape, last_...  1.68 us
    pallas_call x1, Pallas kernels, body(): call(stage_kernel, 'stage', [HBM] * 2, [f32(planes, SUB, LANES), f32(2, p...  1.29 us
    ppermute x1, waiting for transfers between devices, body(): other_curves = lax.ppermute(mine, 'lvl', swap)  1.16 us
    pallas_call x1, Pallas kernels, body(): call(put_mine_kernel, 'put_mine', [VMEM], f32(rows, width), sems, HBM)(mine)  0.84 us
    pallas_call x1, Pallas kernels, body(): call(put_theirs_kernel, 'put_theirs', [VMEM, HBM], f32(rows, width), sems...  0.83 us
  transfers between devices with their start and end apart: 3, of which 3 were waited for; matrix products, arithmetic and copies ran while one was open for 0% of the time, Pallas kernels for 15%

profile of v5, /device:TPU:0, one launch (start us, length us, event | category | flops | bytes accessed | tf_op | source)
XLA Modules:
  0.0 16.4 jit_solution(1025880614779280029)
XLA Ops:
  0.0 1.3 %stage.1 = (f32[32,8,128]{2,1,0:T(8,128)S(1)}, f32[2,32,8,128]{3,2,1,0:T(8,128)S(1)}, f32[24,8,128]{2,1,0:T(8,128)S(1)}, f32[8,17]{1,0:T(8,128)S(1)}, bf16[768,2...) custom-call(f32[256,512]{1,0:T(8,128)} %image_ref.1, ...), custom_call_target="tpu_custom_call" | custom-call | tf_op jit(solution)/shard_map/stage/pallas_call | solution.py:603
  1.3 1.7 %early.1 = (f32[2,8,18,2,8,128]{5,4,3,2,1,0:T(8,128)S(1)}, bf16[2,8,16,768]{3,2,1,0:T(8,128)(2,1)S(1)}, f32[2,32,8,128]{3,2,1,0:T(8,128)S(1)}, f32[2,32,8,128]{3...) custom-call(f32[32,8,128]{2,1,0:T(8,128)S(1)} %get-tuple-element.47., ...), custom_call_target="tpu_custom_call" | custom-call | tf_op jit(solution)/shard_map/early/pallas_call | solution.py:622
  3.0 3.8 %collective-permute-start = (f32[24,8,128]{2,1,0:T(8,128)S(1)}, f32[24,8,128]{2,1,0:T(8,128)S(1)}, u32[]{:S(2)}, u32[]{:S(2)}) collective-permute-start(f32[24,8,128]{2,1,0:T(8,128)S(1)} %get-tuple-element.57), channel_id=1, source_target_pairs={{1,2},{0,15},{3,4},{2,1},{5,6},{4,3},{7,8},{6,5},{9,10},{8,7},{11,... | collective-permute-start | bytes 294920 | tf_op jit(solution)/shard_map/ppermute | solution.py:624
  6.8 0.0 collective-permute-start.1
  6.8 1.2 %collective-permute-done.1.other_ref = f32[8,17]{1,0:T(8,128)S(1)} collective-permute-done((f32[8,17]{1,0:T(8,128)S(1)}, f32[8,17]{1,0:T(8,128)S(1)}, u32[]{:S(2)}, u32[]{:S(2)}) %collective-permute-start.1) | collective-permute-done | bytes 576 | tf_op jit(solution)/shard_map/ppermute | solution.py:625
  8.0 1.7 %other.1 = (f32[2,8,18,2,8,128]{5,4,3,2,1,0:T(8,128)S(1)}, f32[16,11,8,128]{3,2,1,0:T(8,128)S(1)}, bf16[2,8,16,768]{3,2,1,0:T(8,128)(2,1)S(1)}, f32[2,32,8,128]{3,2,1,0:T(8,128)S(1)}) custom-call(f32[32,8,128]{2,1,0:T(8,128)S(1)} %get-tuple-element.47.refs_0_.edge_ref, ...), custom_call_target="tpu_custom_call", output_to_operand_aliasing={{0}: (8, {}), {1}: (9, {})} | custom-call | tf_op jit(solution)/shard_map/other/pallas_call | solution.py:630
  9.7 0.2 %collective-permute-done.halo_ref = f32[24,8,128]{2,1,0:T(8,128)S(1)} collective-permute-done((f32[24,8,128]{2,1,0:T(8,128)S(1)}, f32[24,8,128]{2,1,0:T(8,128)S(1)}, u32[]{:S(2)}, u32[]{:S(2)}) %collective-permute-start) | collective-permute-done | bytes 98336 | tf_op jit(solution)/shard_map/ppermute | solution.py:624
  9.9 4.1 %rest.1 = (f32[2,32,8,128]{3,2,1,0:T(8,128)S(1)}, f32[2,8,18,2,8,128]{5,4,3,2,1,0:T(8,128)S(1)}) custom-call(f32[24,8,128]{2,1,0:T(8,128)S(1)} %collective-permute-done.halo_ref, f32[2,8,18,2,8,128]{5,4,3,2,1,0:T(8,128)S(1)} %get-tuple-element.71.gauss_in_ref, ...), custom_call_target="tpu_custom_call", output_to_operand_aliasing={{1}: (1, {})} | custom-call | tf_op jit(solution)/shard_map/rest/pallas_call | solution.py:634
  14.0 0.1 collective-permute-start.2
  14.1 0.8 %put_mine.1.begun_ref = f32[256,512]{1,0:T(8,128)} custom-call(f32[2,32,8,128]{3,2,1,0:T(8,128)S(1)} %get-tuple-element.84.mine_ref), custom_call_target="tpu_custom_call" | custom-call | tf_op jit(solution)/shard_map/put_mine/pallas_call | solution.py:642
  14.9 0.7 %collective-permute-done.2.theirs_ref = f32[2,32,8,128]{3,2,1,0:T(8,128)S(1)} collective-permute-done((f32[2,32,8,128]{3,2,1,0:T(8,128)S(1)}, f32[2,32,8,128]{3,2,1,0:T(8,128)S(1)}, u32[]{:S(2)}, u32[]{:S(2)}) %collective-permute-start.2) | collective-permute-done | bytes 262176 | tf_op jit(solution)/shard_map/ppermute | solution.py:640
  15.6 0.8 %put_theirs.1 = f32[256,512]{1,0:T(8,128)} custom-call(f32[2,32,8,128]{3,2,1,0:T(8,128)S(1)} %collective-permute-done.2.theirs_ref, f32[256,512]{1,0:T(8,128)} %put_mine.1.begun_ref), custom_call_target="tpu_custom_call", output_to_operand_aliasing={{}: (1, {})} | custom-call | tf_op jit(solution)/shard_map/put_theirs/pallas_call | solution.py:643
  (1 shorter events, 0.0 us)
Async XLA Ops:
  3.0 6.8 %collective-permute-start = (f32[24,8,128]{2,1,0:T(8,128)S(1)}, f32[24,8,128]{2,1,0:T(8,128)S(1)}, u32[]{:S(2)}, u32[]{:S(2)}) collective-permute-start(f32[24,8,128]{2,1,0:T(8,128)S(1)} %get-tuple-element.57), channel_id=1, source_target_pairs={{1,2},{0,15},{3,4},{2,1},{5,6},{4,3},{7,8},{6,5},{9,10},{8,7},{11,... | collective-permute-start | bytes 294920 | tf_op jit(solution)/shard_map/ppermute | solution.py:624
  6.8 1.2 %collective-permute-start.1 = (f32[8,17]{1,0:T(8,128)S(1)}, f32[8,17]{1,0:T(8,128)S(1)}, u32[]{:S(2)}, u32[]{:S(2)}) collective-permute-start(f32[8,17]{1,0:T(8,128)S(1)} %get-tuple-element.58.refs_2_.mine_ref), channel_id=1, source_target_pairs={{0,1},{1,0},{2,3},{3,2},{4,5},{5,4},{6,7},{7,6},{8,9},{9,8},{10,11... | collective-permute-start | bytes 1640 | tf_op jit(solution)/shard_map/ppermute | solution.py:625
  14.0 1.6 %collective-permute-start.2 = (f32[2,32,8,128]{3,2,1,0:T(8,128)S(1)}, f32[2,32,8,128]{3,2,1,0:T(8,128)S(1)}, u32[]{:S(2)}, u32[]{:S(2)}) collective-permute-start(f32[2,32,8,128]{3,2,1,0:T(8,128)S(1)} %get-tuple-element.84.mine_ref), channel_id=1, source_target_pairs={{0,1},{1,0},{2,3},{3,2},{4,5},{5,4},{6,7},{7,6},{8,9},{9,8},{10,11... | collective-permute-start | bytes 786440 | tf_op jit(solution)/shard_map/ppermute | solution.py:640

commit v6 on v5

--- a/solution.py
+++ b/solution.py
@@ -119,7 +119,7 @@
 
 
 def by_lane(p):
-    return p % 4 == 1
+    return p % 4 == 2
 
 
 def curve_cell(p, x):
@@ -266,13 +266,12 @@
     planes = edge_ref.shape[0]
     half = 2 * LANES
     outermost = pl.multiple_of(lvl * 3 * LANES, LANES)
-    pairs = [(curves_ref, mine_ref)]
-    for q in range(SUB):
-        rows = pl.ds(q * planes, planes)
-        pairs.append((image_ref.at[rows, pl.ds(outermost, LANES)], edge_ref.at[:, q, :]))
-        for tile in range(2):
-            source = image_ref.at[rows, (tile + 1) * LANES:(tile + 2) * LANES]
-            pairs.append((source, inner_ref.at[tile, :, q, :]))
+    rows = [pl.ds(q * planes, planes) for q in range(SUB)]
+    pairs = [(image_ref.at[rows[q], pl.ds(outermost, LANES)], edge_ref.at[:, q, :]) for q in range(SUB)]
+    pairs.append((curves_ref, mine_ref))
+    for tile in range(2):
+        columns = slice((tile + 1) * LANES, (tile + 2) * LANES)
+        pairs += [(image_ref.at[rows[q], columns], inner_ref.at[tile, :, q, :]) for q in range(SUB)]
     copies = start_all(pairs, sems)
 
     def put(ref, shape, value):
@@ -311,12 +310,13 @@
     put(away_ref, (LANES, half), up_pair(away_column, 1))
     put(narrow_ref, (LANES, half), lambda i, j: up_taps(2 * i - level_one_column(lvl, j)))
     put(raise_ref, (LANES, LANES), lambda i, j: up_taps(2 * i - j))
-    wait_all(copies)
+    wait_all(copies[:SUB])
     kept = kept_lanes(lvl)
     for group in range(planes // 4):
         *three, fourth = [edge_ref[4 * group + at] for at in range(4)]
         for at, x in enumerate(three):
             sent_ref[3 * group + at] = jnp.where(kept, x, pltpu.roll(fourth, LANES - PIECE * (at + 1), axis=1))
+    wait_all(copies[SUB:])
 
 
 def put_kernel(half_ref, out_ref, sems, lvl):
@@ -541,11 +541,11 @@
         here = gauss[level][p]
         return pick(*scaled_level(here[0]), lambda k: here[FIRST + k] - raised[p][k])
 
+    columns_up(1)
     lift = raise_ref[...]
     gauss = [None, [level_one(p) for p in range(planes // 2)]]
     gauss.append(next_level(gauss[1], wide_ref[...]))
     raised = [None, raise_stack(gauss[2], narrow_ref[...])]
-    columns_up(1)
     columns_up(0)
     coeffs = [None, []]
     quarter = planes // 8

time: 16.6 us -> 16 us (0.964)
  Pallas kernels: 10.5 us -> 9.87 us
    pallas_call x1, Pallas kernels: 4.12 us -> 3.69 us  [body(): call(rest_kernel, 'rest', [VMEM] * 15, [out_shape, gauss_shape], [fast_in...]
  transfers between devices with their start and end apart: 3 -> 3, of which waited for: 3 -> 3; matrix products, arithmetic and copies ran while one was open for 0% -> 0% of each run, Pallas kernels for 15% -> 16%
where the time goes in v6:
time: 16 us; the launch traced here: 15.8 us
  Pallas kernels  9.87 us (62%)
  starting transfers between devices  3.93 us (25%)
  waiting for transfers between devices  2.01 us (13%)
    ppermute x1, starting transfers between devices, body(): halo = lax.ppermute(sent, ('tile', 'lvl'), pairs)  3.84 us
    pallas_call x1, Pallas kernels, body(): call(rest_kernel, 'rest', [VMEM] * 15, [out_shape, gauss_shape], [fast_in...  3.69 us
    pallas_call x1, Pallas kernels, body(): call(early_kernel, 'early', [VMEM] * 4, own_shapes, part)  1.7 us
    pallas_call x1, Pallas kernels, body(): call(other_kernel, 'other', [VMEM] * 10, [gauss_shape, table_shape, last_...  1.62 us
    pallas_call x1, Pallas kernels, body(): call(stage_kernel, 'stage', [HBM] * 2, [f32(planes, SUB, LANES), f32(2, p...  1.19 us
    ppermute x1, waiting for transfers between devices, body(): other_curves = lax.ppermute(mine, 'lvl', swap)  1.16 us
    pallas_call x1, Pallas kernels, body(): call(put_mine_kernel, 'put_mine', [VMEM], f32(rows, width), sems, HBM)(mine)  0.83 us
    pallas_call x1, Pallas kernels, body(): call(put_theirs_kernel, 'put_theirs', [VMEM, HBM], f32(rows, width), sems...  0.83 us
  transfers between devices with their start and end apart: 3, of which 3 were waited for; matrix products, arithmetic and copies ran while one was open for 0% of the time, Pallas kernels for 16%

profile of v6, /device:TPU:0, one launch (start us, length us, event | category | flops | bytes accessed | tf_op | source)
XLA Modules:
  0.0 15.8 jit_solution(11304496441361804906)
XLA Ops:
  0.0 1.2 %stage.1 = (f32[32,8,128]{2,1,0:T(8,128)S(1)}, f32[2,32,8,128]{3,2,1,0:T(8,128)S(1)}, f32[24,8,128]{2,1,0:T(8,128)S(1)}, f32[8,17]{1,0:T(8,128)S(1)}, bf16[768,2...) custom-call(f32[256,512]{1,0:T(8,128)} %image_ref.1, ...), custom_call_target="tpu_custom_call" | custom-call | tf_op jit(solution)/shard_map/stage/pallas_call | solution.py:603
  1.2 1.7 %early.1 = (f32[2,8,18,2,8,128]{5,4,3,2,1,0:T(8,128)S(1)}, bf16[2,8,16,768]{3,2,1,0:T(8,128)(2,1)S(1)}, f32[2,32,8,128]{3,2,1,0:T(8,128)S(1)}, f32[2,32,8,128]{3...) custom-call(f32[32,8,128]{2,1,0:T(8,128)S(1)} %get-tuple-element.47., ...), custom_call_target="tpu_custom_call" | custom-call | tf_op jit(solution)/shard_map/early/pallas_call | solution.py:622
  2.9 3.8 %collective-permute-start = (f32[24,8,128]{2,1,0:T(8,128)S(1)}, f32[24,8,128]{2,1,0:T(8,128)S(1)}, u32[]{:S(2)}, u32[]{:S(2)}) collective-permute-start(f32[24,8,128]{2,1,0:T(8,128)S(1)} %get-tuple-element.57), channel_id=1, source_target_pairs={{1,2},{0,15},{3,4},{2,1},{5,6},{4,3},{7,8},{6,5},{9,10},{8,7},{11,... | collective-permute-start | bytes 294920 | tf_op jit(solution)/shard_map/ppermute | solution.py:624
  6.8 0.0 collective-permute-start.1
  6.8 1.2 %collective-permute-done.1.other_ref = f32[8,17]{1,0:T(8,128)S(1)} collective-permute-done((f32[8,17]{1,0:T(8,128)S(1)}, f32[8,17]{1,0:T(8,128)S(1)}, u32[]{:S(2)}, u32[]{:S(2)}) %collective-permute-start.1) | collective-permute-done | bytes 576 | tf_op jit(solution)/shard_map/ppermute | solution.py:625
  7.9 1.6 %other.1 = (f32[2,8,18,2,8,128]{5,4,3,2,1,0:T(8,128)S(1)}, f32[16,11,8,128]{3,2,1,0:T(8,128)S(1)}, bf16[2,8,16,768]{3,2,1,0:T(8,128)(2,1)S(1)}, f32[2,32,8,128]{3,2,1,0:T(8,128)S(1)}) custom-call(f32[32,8,128]{2,1,0:T(8,128)S(1)} %get-tuple-element.47.refs_0_.edge_ref, ...), custom_call_target="tpu_custom_call", output_to_operand_aliasing={{0}: (8, {}), {1}: (9, {})} | custom-call | tf_op jit(solution)/shard_map/other/pallas_call | solution.py:630
  9.6 0.2 %collective-permute-done.halo_ref = f32[24,8,128]{2,1,0:T(8,128)S(1)} collective-permute-done((f32[24,8,128]{2,1,0:T(8,128)S(1)}, f32[24,8,128]{2,1,0:T(8,128)S(1)}, u32[]{:S(2)}, u32[]{:S(2)}) %collective-permute-start) | collective-permute-done | bytes 98336 | tf_op jit(solution)/shard_map/ppermute | solution.py:624
  9.7 3.7 %rest.1 = (f32[2,32,8,128]{3,2,1,0:T(8,128)S(1)}, f32[2,8,18,2,8,128]{5,4,3,2,1,0:T(8,128)S(1)}) custom-call(f32[24,8,128]{2,1,0:T(8,128)S(1)} %collective-permute-done.halo_ref, f32[2,8,18,2,8,128]{5,4,3,2,1,0:T(8,128)S(1)} %get-tuple-element.71.gauss_in_ref, ...), custom_call_target="tpu_custom_call", output_to_operand_aliasing={{1}: (1, {})} | custom-call | tf_op jit(solution)/shard_map/rest/pallas_call | solution.py:634
  13.4 0.1 collective-permute-start.2
  13.5 0.8 %put_mine.1.begun_ref = f32[256,512]{1,0:T(8,128)} custom-call(f32[2,32,8,128]{3,2,1,0:T(8,128)S(1)} %get-tuple-element.84.mine_ref), custom_call_target="tpu_custom_call" | custom-call | tf_op jit(solution)/shard_map/put_mine/pallas_call | solution.py:642
  14.3 0.7 %collective-permute-done.2.theirs_ref = f32[2,32,8,128]{3,2,1,0:T(8,128)S(1)} collective-permute-done((f32[2,32,8,128]{3,2,1,0:T(8,128)S(1)}, f32[2,32,8,128]{3,2,1,0:T(8,128)S(1)}, u32[]{:S(2)}, u32[]{:S(2)}) %collective-permute-start.2) | collective-permute-done | bytes 262176 | tf_op jit(solution)/shard_map/ppermute | solution.py:640
  15.0 0.8 %put_theirs.1 = f32[256,512]{1,0:T(8,128)} custom-call(f32[2,32,8,128]{3,2,1,0:T(8,128)S(1)} %collective-permute-done.2.theirs_ref, f32[256,512]{1,0:T(8,128)} %put_mine.1.begun_ref), custom_call_target="tpu_custom_call", output_to_operand_aliasing={{}: (1, {})} | custom-call | tf_op jit(solution)/shard_map/put_theirs/pallas_call | solution.py:643
  (1 shorter events, 0.0 us)
Async XLA Ops:
  2.9 6.8 %collective-permute-start = (f32[24,8,128]{2,1,0:T(8,128)S(1)}, f32[24,8,128]{2,1,0:T(8,128)S(1)}, u32[]{:S(2)}, u32[]{:S(2)}) collective-permute-start(f32[24,8,128]{2,1,0:T(8,128)S(1)} %get-tuple-element.57), channel_id=1, source_target_pairs={{1,2},{0,15},{3,4},{2,1},{5,6},{4,3},{7,8},{6,5},{9,10},{8,7},{11,... | collective-permute-start | bytes 294920 | tf_op jit(solution)/shard_map/ppermute | solution.py:624
  6.8 1.2 %collective-permute-start.1 = (f32[8,17]{1,0:T(8,128)S(1)}, f32[8,17]{1,0:T(8,128)S(1)}, u32[]{:S(2)}, u32[]{:S(2)}) collective-permute-start(f32[8,17]{1,0:T(8,128)S(1)} %get-tuple-element.58.refs_2_.mine_ref), channel_id=1, source_target_pairs={{0,1},{1,0},{2,3},{3,2},{4,5},{5,4},{6,7},{7,6},{8,9},{9,8},{10,11... | collective-permute-start | bytes 1640 | tf_op jit(solution)/shard_map/ppermute | solution.py:625
  13.4 1.6 %collective-permute-start.2 = (f32[2,32,8,128]{3,2,1,0:T(8,128)S(1)}, f32[2,32,8,128]{3,2,1,0:T(8,128)S(1)}, u32[]{:S(2)}, u32[]{:S(2)}) collective-permute-start(f32[2,32,8,128]{3,2,1,0:T(8,128)S(1)} %get-tuple-element.84.mine_ref), channel_id=1, source_target_pairs={{0,1},{1,0},{2,3},{3,2},{4,5},{5,4},{6,7},{7,6},{8,9},{9,8},{10,11... | collective-permute-start | bytes 786440 | tf_op jit(solution)/shard_map/ppermute | solution.py:640

commit v7 on v6

--- a/solution.py
+++ b/solution.py
@@ -378,13 +378,12 @@
             gauss_ref[tile, :, target + copy] = result[copy, :, :, :, span]
 
 
-def own_pairs(table_ref, first, cell_ref, fraction_ref, down_ref, gauss_ref, last_ref, part_scr, before):
+def own_pairs(steps, table_ref, first, cell_ref, fraction_ref, down_ref, gauss_ref, last_ref, part_scr, before):
     planes = cell_ref.shape[1]
-    pairs = LEVELS // 4
     waiting = before
-    for step in range(pairs):
+    for step in steps:
         multiply_own(waiting[0], down_ref, gauss_ref, waiting[1])
-        ref = last_ref if step == pairs - 1 else part_scr.at[step % 2]
+        ref = last_ref if step == steps[-1] else part_scr.at[step % 2]
         for tile in range(3):
             mapped = remap_pair(
                 table_ref, first + 2 * step, planes, lambda p: cell_ref[tile, p], lambda p: fraction_ref[tile, p]
@@ -399,20 +398,42 @@
     return (lax.axis_index("tile") == 0) & foremost
 
 
+def waits_for_both():
+    return waits_longest() & (lax.axis_index("lvl") == 1)
+
+
 def early_kernel(*refs):
     @pl.when(waits_longest())
     def _():
-        mine_part(*refs)
+        mine_begin(*refs)
+
+    @pl.when(waits_for_both())
+    def _():
+        mine_end(*refs)
 
 
 def late_kernel(*refs):
+    refs = refs[:4] + refs[11:]
+
     @pl.when(jnp.logical_not(waits_longest()))
     def _():
-        mine_part(*refs[:4], *refs[11:])
-
-
-def mine_part(edge_ref, inner_ref, mine_ref, down_ref, gauss_ref, last_ref, place_ref, weight_ref,
-                table_ref, cell_ref, fraction_ref, part_scr):
+        mine_begin(*refs)
+
+    @pl.when(jnp.logical_not(waits_for_both()))
+    def _():
+        mine_end(*refs)
+
+
+def mine_end(edge_ref, inner_ref, mine_ref, down_ref, gauss_ref, last_ref, place_ref, weight_ref,
+             table_ref, cell_ref, fraction_ref, part_scr):
+    first = lax.axis_index("lvl") * (LEVELS // 2)
+    steps = range(LEVELS // 8, LEVELS // 4)
+    before = (last_ref, FIRST + first + 2 * (steps[0] - 1))
+    own_pairs(steps, table_ref, first, cell_ref, fraction_ref, down_ref, gauss_ref, last_ref, part_scr, before)
+
+
+def mine_begin(edge_ref, inner_ref, mine_ref, down_ref, gauss_ref, last_ref, place_ref, weight_ref,
+               table_ref, cell_ref, fraction_ref, part_scr):
     planes = edge_ref.shape[0]
     first = lax.axis_index("lvl") * (LEVELS // 2)
     all_tables(table_ref, mine_ref, first)
@@ -427,7 +448,8 @@
         for copy in range(2):
             split_store(part_scr.at[1, copy], reduced, tile * LANES, 3 * LANES)
     before = (part_scr.at[1], 0)
-    own_pairs(table_ref, first, cell_ref, fraction_ref, down_ref, gauss_ref, last_ref, part_scr, before)
+    steps = range(LEVELS // 8)
+    own_pairs(steps, table_ref, first, cell_ref, fraction_ref, down_ref, gauss_ref, last_ref, part_scr, before)
 
 
 def other_kernel(edge_ref, inner_ref, mine_ref, other_ref, down_ref, cell_ref, fraction_ref, last_in_ref,
@@ -442,7 +464,8 @@
         for p in range(edge_ref.shape[0]):
             tone_ref[tile, p] = tone(tones, image_of(edge_ref, inner_ref, tile, p))
     before = (last_in_ref, FIRST + lvl * (LEVELS // 2) + LEVELS // 2 - 2)
-    own_pairs(table_ref, first, cell_ref, fraction_ref, down_ref, gauss_ref, last_ref, part_scr, before)
+    steps = range(LEVELS // 4)
+    own_pairs(steps, table_ref, first, cell_ref, fraction_ref, down_ref, gauss_ref, last_ref, part_scr, before)
 
 
 def rest_kernel(halo_ref, gauss_in_ref, last_ref, tone_ref, place_ref, weight_ref, table_ref, down_ref,

time: 16 us -> 15.9 us (level)
  waiting for transfers between devices: 2.01 us -> 1 us
  starting transfers between devices: 3.93 us -> 4.73 us
    ppermute x1, waiting for transfers between devices: 1.16 us -> 0.46 us  [body(): other_curves = lax.ppermute(mine, 'lvl', swap)]
    pallas_call x1, Pallas kernels: 0.01 us -> 0.69 us  [body(): call(late_kernel, 'late', [VMEM] * 11, own_shapes, part, input_output_ali...]
    ppermute x1, starting transfers between devices: 3.84 us -> 4.5 us  [body(): halo = lax.ppermute(sent, ('tile', 'lvl'), pairs)]
    pallas_call x1, Pallas kernels: 1.7 us -> 1.05 us  [body(): call(early_kernel, 'early', [VMEM] * 4, own_shapes, part)]
    ppermute x1, waiting for transfers between devices: 0.17 us -> 0.01 us  [body(): halo = lax.ppermute(sent, ('tile', 'lvl'), pairs)]
  transfers between devices with their start and end apart: 3 -> 3, of which waited for: 3 -> 2; matrix products, arithmetic and copies ran while one was open for 0% -> 0% of each run, Pallas kernels for 16% -> 20%
where the time goes in v7:
time: 15.9 us; the launch traced here: 15.7 us
  Pallas kernels  9.91 us (62%)
  starting transfers between devices  4.73 us (30%)
  waiting for transfers between devices  1 us (6%)
    ppermute x1, starting transfers between devices, body(): halo = lax.ppermute(sent, ('tile', 'lvl'), pairs)  4.5 us
    pallas_call x1, Pallas kernels, body(): call(rest_kernel, 'rest', [VMEM] * 15, [out_shape, gauss_shape], [fast_in...  3.7 us
    pallas_call x1, Pallas kernels, body(): call(other_kernel, 'other', [VMEM] * 10, [gauss_shape, table_shape, last_...  1.62 us
    pallas_call x1, Pallas kernels, body(): call(stage_kernel, 'stage', [HBM] * 2, [f32(planes, SUB, LANES), f32(2, p...  1.19 us
    pallas_call x1, Pallas kernels, body(): call(early_kernel, 'early', [VMEM] * 4, own_shapes, part)  1.05 us
    pallas_call x1, Pallas kernels, body(): call(put_theirs_kernel, 'put_theirs', [VMEM, HBM], f32(rows, width), sems...  0.83 us
    pallas_call x1, Pallas kernels, body(): call(put_mine_kernel, 'put_mine', [VMEM], f32(rows, width), sems, HBM)(mine)  0.83 us
    pallas_call x1, Pallas kernels, body(): call(late_kernel, 'late', [VMEM] * 11, own_shapes, part, input_output_ali...  0.69 us
  transfers between devices with their start and end apart: 3, of which 2 were waited for; matrix products, arithmetic and copies ran while one was open for 0% of the time, Pallas kernels for 20%

profile of v7, /device:TPU:0, one launch (start us, length us, event | category | flops | bytes accessed | tf_op | source)
XLA Modules:
  0.0 15.7 jit_solution(5023271821740581133)
XLA Ops:
  0.0 1.2 %stage.1 = (f32[32,8,128]{2,1,0:T(8,128)S(1)}, f32[2,32,8,128]{3,2,1,0:T(8,128)S(1)}, f32[24,8,128]{2,1,0:T(8,128)S(1)}, f32[8,17]{1,0:T(8,128)S(1)}, bf16[768,2...) custom-call(f32[256,512]{1,0:T(8,128)} %image_ref.1, ...), custom_call_target="tpu_custom_call" | custom-call | tf_op jit(solution)/shard_map/stage/pallas_call | solution.py:626
  1.2 1.0 %early.1 = (f32[2,8,18,2,8,128]{5,4,3,2,1,0:T(8,128)S(1)}, bf16[2,8,16,768]{3,2,1,0:T(8,128)(2,1)S(1)}, f32[2,32,8,128]{3,2,1,0:T(8,128)S(1)}, f32[2,32,8,128]{3...) custom-call(f32[32,8,128]{2,1,0:T(8,128)S(1)} %get-tuple-element.47., ...), custom_call_target="tpu_custom_call" | custom-call | tf_op jit(solution)/shard_map/early/pallas_call | solution.py:645
  2.3 4.5 %collective-permute-start = (f32[24,8,128]{2,1,0:T(8,128)S(1)}, f32[24,8,128]{2,1,0:T(8,128)S(1)}, u32[]{:S(2)}, u32[]{:S(2)}) collective-permute-start(f32[24,8,128]{2,1,0:T(8,128)S(1)} %get-tuple-element.57), channel_id=1, source_target_pairs={{1,2},{0,15},{3,4},{2,1},{5,6},{4,3},{7,8},{6,5},{9,10},{8,7},{11,... | collective-permute-start | bytes 294920 | tf_op jit(solution)/shard_map/ppermute | solution.py:647
  6.8 0.0 collective-permute-start.1
  6.8 0.7 %late.1 = (f32[2,8,18,2,8,128]{5,4,3,2,1,0:T(8,128)S(1)}, bf16[2,8,16,768]{3,2,1,0:T(8,128)(2,1)S(1)}, f32[2,32,8,128]{3,2,1,0:T(8,128)S(1)}, f32[2,32,8,128]{3,...) custom-call(f32[32,8,128]{2,1,0:T(8,128)S(1)} %get-tuple-element.47., ...), custom_call_target="tpu_custom_call", output_to_operand_aliasing={{0}: (4, {}), {1}: (5, {}), {2}: (6, {}), {3}: (7, {}), {4}... | custom-call | tf_op jit(solution)/shard_map/late/pallas_call | solution.py:649
  7.5 0.5 %collective-permute-done.1.other_ref = f32[8,17]{1,0:T(8,128)S(1)} collective-permute-done((f32[8,17]{1,0:T(8,128)S(1)}, f32[8,17]{1,0:T(8,128)S(1)}, u32[]{:S(2)}, u32[]{:S(2)}) %collective-permute-start.1) | collective-permute-done | bytes 576 | tf_op jit(solution)/shard_map/ppermute | solution.py:648
  7.9 1.6 %other.1 = (f32[2,8,18,2,8,128]{5,4,3,2,1,0:T(8,128)S(1)}, f32[16,11,8,128]{3,2,1,0:T(8,128)S(1)}, bf16[2,8,16,768]{3,2,1,0:T(8,128)(2,1)S(1)}, f32[2,32,8,128]{3,2,1,0:T(8,128)S(1)}) custom-call(f32[32,8,128]{2,1,0:T(8,128)S(1)} %get-tuple-element.47.refs_0_.edge_ref, ...), custom_call_target="tpu_custom_call", output_to_operand_aliasing={{0}: (8, {}), {1}: (9, {})} | custom-call | tf_op jit(solution)/shard_map/other/pallas_call | solution.py:653
  9.6 0.0 collective-permute-done.halo_ref
  9.6 3.7 %rest.1 = (f32[2,32,8,128]{3,2,1,0:T(8,128)S(1)}, f32[2,8,18,2,8,128]{5,4,3,2,1,0:T(8,128)S(1)}) custom-call(f32[24,8,128]{2,1,0:T(8,128)S(1)} %collective-permute-done.halo_ref, f32[2,8,18,2,8,128]{5,4,3,2,1,0:T(8,128)S(1)} %get-tuple-element.71.gauss_in_ref, ...), custom_call_target="tpu_custom_call", output_to_operand_aliasing={{1}: (1, {})} | custom-call | tf_op jit(solution)/shard_map/rest/pallas_call | solution.py:657
  13.3 0.2 %collective-permute-start.2 = (f32[2,32,8,128]{3,2,1,0:T(8,128)S(1)}, f32[2,32,8,128]{3,2,1,0:T(8,128)S(1)}, u32[]{:S(2)}, u32[]{:S(2)}) collective-permute-start(f32[2,32,8,128]{3,2,1,0:T(8,128)S(1)} %get-tuple-element.84.mine_ref), channel_id=1, source_target_pairs={{0,1},{1,0},{2,3},{3,2},{4,5},{5,4},{6,7},{7,6},{8,9},{9,8},{10,11... | collective-permute-start | bytes 786440 | tf_op jit(solution)/shard_map/ppermute | solution.py:663
  13.5 0.8 %put_mine.1.begun_ref = f32[256,512]{1,0:T(8,128)} custom-call(f32[2,32,8,128]{3,2,1,0:T(8,128)S(1)} %get-tuple-element.84.mine_ref), custom_call_target="tpu_custom_call" | custom-call | tf_op jit(solution)/shard_map/put_mine/pallas_call | solution.py:665
  14.3 0.5 %collective-permute-done.2.theirs_ref = f32[2,32,8,128]{3,2,1,0:T(8,128)S(1)} collective-permute-done((f32[2,32,8,128]{3,2,1,0:T(8,128)S(1)}, f32[2,32,8,128]{3,2,1,0:T(8,128)S(1)}, u32[]{:S(2)}, u32[]{:S(2)}) %collective-permute-start.2) | collective-permute-done | bytes 262176 | tf_op jit(solution)/shard_map/ppermute | solution.py:663
  14.9 0.8 %put_theirs.1 = f32[256,512]{1,0:T(8,128)} custom-call(f32[2,32,8,128]{3,2,1,0:T(8,128)S(1)} %collective-permute-done.2.theirs_ref, f32[256,512]{1,0:T(8,128)} %put_mine.1.begun_ref), custom_call_target="tpu_custom_call", output_to_operand_aliasing={{}: (1, {})} | custom-call | tf_op jit(solution)/shard_map/put_theirs/pallas_call | solution.py:666
Async XLA Ops:
  2.3 7.3 %collective-permute-start = (f32[24,8,128]{2,1,0:T(8,128)S(1)}, f32[24,8,128]{2,1,0:T(8,128)S(1)}, u32[]{:S(2)}, u32[]{:S(2)}) collective-permute-start(f32[24,8,128]{2,1,0:T(8,128)S(1)} %get-tuple-element.57), channel_id=1, source_target_pairs={{1,2},{0,15},{3,4},{2,1},{5,6},{4,3},{7,8},{6,5},{9,10},{8,7},{11,... | collective-permute-start | bytes 294920 | tf_op jit(solution)/shard_map/ppermute | solution.py:647
  6.8 1.2 %collective-permute-start.1 = (f32[8,17]{1,0:T(8,128)S(1)}, f32[8,17]{1,0:T(8,128)S(1)}, u32[]{:S(2)}, u32[]{:S(2)}) collective-permute-start(f32[8,17]{1,0:T(8,128)S(1)} %get-tuple-element.58.refs_2_.mine_ref), channel_id=1, source_target_pairs={{0,1},{1,0},{2,3},{3,2},{4,5},{5,4},{6,7},{7,6},{8,9},{9,8},{10,11... | collective-permute-start | bytes 1640 | tf_op jit(solution)/shard_map/ppermute | solution.py:648
  13.3 1.6 %collective-permute-start.2 = (f32[2,32,8,128]{3,2,1,0:T(8,128)S(1)}, f32[2,32,8,128]{3,2,1,0:T(8,128)S(1)}, u32[]{:S(2)}, u32[]{:S(2)}) collective-permute-start(f32[2,32,8,128]{3,2,1,0:T(8,128)S(1)} %get-tuple-element.84.mine_ref), channel_id=1, source_target_pairs={{0,1},{1,0},{2,3},{3,2},{4,5},{5,4},{6,7},{7,6},{8,9},{9,8},{10,11... | collective-permute-start | bytes 786440 | tf_op jit(solution)/shard_map/ppermute | solution.py:663

commit v8 on v7

--- a/solution.py
+++ b/solution.py
@@ -538,13 +538,15 @@
             level_zero(*waiting.pop(0))
 
     def level_one(p):
-        return jnp.concatenate([gauss_ref[tile, p // 2, :, p % 2] for tile in range(2)], axis=-1)
+        guide = [gauss_ref[tile, p // 2, 0:1, p % 2] for tile in range(2)]
+        copies = [gauss_ref[tile, p // 2, FIRST:, p % 2] for tile in range(2)]
+        return jnp.concatenate([jnp.concatenate(part, axis=-1) for part in (guide, copies)], axis=0)
 
     def next_level(coarse, table):
         reduced = rows_down(coarse)
         stacked = jnp.concatenate(reduced, axis=0)
         result = dot(halves(stacked.reshape(-1, stacked.shape[-1])), table)
-        result = result.reshape(len(reduced), STACK, SUB, LANES)
+        result = result.reshape(len(reduced), 1 + LEVELS, SUB, LANES)
         return [result[p] for p in range(len(reduced))]
 
     def raise_columns(stacks, table):
@@ -553,7 +555,7 @@
         return result.reshape((len(stacks), -1, SUB, table.shape[1]))
 
     def raise_stack(coarse, table):
-        result = raise_columns([plane[FIRST:] for plane in coarse], table)
+        result = raise_columns([plane[1:] for plane in coarse], table)
         return rows_up([result[p] for p in range(len(coarse))])
 
     def raise_one(planes_of, table):
@@ -562,7 +564,7 @@
 
     def coefficient(level, raised, p):
         here = gauss[level][p]
-        return pick(*scaled_level(here[0]), lambda k: here[FIRST + k] - raised[p][k])
+        return pick(*scaled_level(here[0]), lambda k: here[1 + k] - raised[p][k])
 
     columns_up(1)
     lift = raise_ref[...]

time: 15.9 us -> 15.8 us (level)
  no operation moved by 1% of the time
where the time goes in v8:
time: 15.8 us; the launch traced here: 15.7 us
  Pallas kernels  9.87 us (62%)
  starting transfers between devices  4.73 us (30%)
  waiting for transfers between devices  1 us (6%)
    ppermute x1, starting transfers between devices, body(): halo = lax.ppermute(sent, ('tile', 'lvl'), pairs)  4.5 us
    pallas_call x1, Pallas kernels, body(): call(rest_kernel, 'rest', [VMEM] * 15, [out_shape, gauss_shape], [fast_in...  3.66 us
    pallas_call x1, Pallas kernels, body(): call(other_kernel, 'other', [VMEM] * 10, [gauss_shape, table_shape, last_...  1.62 us
    pallas_call x1, Pallas kernels, body(): call(stage_kernel, 'stage', [HBM] * 2, [f32(planes, SUB, LANES), f32(2, p...  1.19 us
    pallas_call x1, Pallas kernels, body(): call(early_kernel, 'early', [VMEM] * 4, own_shapes, part)  1.05 us
    pallas_call x1, Pallas kernels, body(): call(put_theirs_kernel, 'put_theirs', [VMEM, HBM], f32(rows, width), sems...  0.83 us
    pallas_call x1, Pallas kernels, body(): call(put_mine_kernel, 'put_mine', [VMEM], f32(rows, width), sems, HBM)(mine)  0.83 us
    pallas_call x1, Pallas kernels, body(): call(late_kernel, 'late', [VMEM] * 11, own_shapes, part, input_output_ali...  0.69 us
  transfers between devices with their start and end apart: 3, of which 2 were waited for; matrix products, arithmetic and copies ran while one was open for 0% of the time, Pallas kernels for 20%

profile of v8, /device:TPU:0, one launch (start us, length us, event | category | flops | bytes accessed | tf_op | source)
XLA Modules:
  0.0 15.7 jit_solution(13100322690723063137)
XLA Ops:
  0.0 1.2 %stage.1 = (f32[32,8,128]{2,1,0:T(8,128)S(1)}, f32[2,32,8,128]{3,2,1,0:T(8,128)S(1)}, f32[24,8,128]{2,1,0:T(8,128)S(1)}, f32[8,17]{1,0:T(8,128)S(1)}, bf16[768,2...) custom-call(f32[256,512]{1,0:T(8,128)} %image_ref.1, ...), custom_call_target="tpu_custom_call" | custom-call | tf_op jit(solution)/shard_map/stage/pallas_call | solution.py:628
  1.2 1.0 %early.1 = (f32[2,8,18,2,8,128]{5,4,3,2,1,0:T(8,128)S(1)}, bf16[2,8,16,768]{3,2,1,0:T(8,128)(2,1)S(1)}, f32[2,32,8,128]{3,2,1,0:T(8,128)S(1)}, f32[2,32,8,128]{3...) custom-call(f32[32,8,128]{2,1,0:T(8,128)S(1)} %get-tuple-element.47., ...), custom_call_target="tpu_custom_call" | custom-call | tf_op jit(solution)/shard_map/early/pallas_call | solution.py:647
  2.3 4.5 %collective-permute-start = (f32[24,8,128]{2,1,0:T(8,128)S(1)}, f32[24,8,128]{2,1,0:T(8,128)S(1)}, u32[]{:S(2)}, u32[]{:S(2)}) collective-permute-start(f32[24,8,128]{2,1,0:T(8,128)S(1)} %get-tuple-element.57), channel_id=1, source_target_pairs={{1,2},{0,15},{3,4},{2,1},{5,6},{4,3},{7,8},{6,5},{9,10},{8,7},{11,... | collective-permute-start | bytes 294920 | tf_op jit(solution)/shard_map/ppermute | solution.py:649
  6.8 0.0 collective-permute-start.1
  6.8 0.7 %late.1 = (f32[2,8,18,2,8,128]{5,4,3,2,1,0:T(8,128)S(1)}, bf16[2,8,16,768]{3,2,1,0:T(8,128)(2,1)S(1)}, f32[2,32,8,128]{3,2,1,0:T(8,128)S(1)}, f32[2,32,8,128]{3,...) custom-call(f32[32,8,128]{2,1,0:T(8,128)S(1)} %get-tuple-element.47., ...), custom_call_target="tpu_custom_call", output_to_operand_aliasing={{0}: (4, {}), {1}: (5, {}), {2}: (6, {}), {3}: (7, {}), {4}... | custom-call | tf_op jit(solution)/shard_map/late/pallas_call | solution.py:651
  7.5 0.5 %collective-permute-done.1.other_ref = f32[8,17]{1,0:T(8,128)S(1)} collective-permute-done((f32[8,17]{1,0:T(8,128)S(1)}, f32[8,17]{1,0:T(8,128)S(1)}, u32[]{:S(2)}, u32[]{:S(2)}) %collective-permute-start.1) | collective-permute-done | bytes 576 | tf_op jit(solution)/shard_map/ppermute | solution.py:650
  7.9 1.6 %other.1 = (f32[2,8,18,2,8,128]{5,4,3,2,1,0:T(8,128)S(1)}, f32[16,11,8,128]{3,2,1,0:T(8,128)S(1)}, bf16[2,8,16,768]{3,2,1,0:T(8,128)(2,1)S(1)}, f32[2,32,8,128]{3,2,1,0:T(8,128)S(1)}) custom-call(f32[32,8,128]{2,1,0:T(8,128)S(1)} %get-tuple-element.47.refs_0_.edge_ref, ...), custom_call_target="tpu_custom_call", output_to_operand_aliasing={{0}: (8, {}), {1}: (9, {})} | custom-call | tf_op jit(solution)/shard_map/other/pallas_call | solution.py:655
  9.6 0.0 collective-permute-done.halo_ref
  9.6 3.7 %rest.1 = (f32[2,32,8,128]{3,2,1,0:T(8,128)S(1)}, f32[2,8,18,2,8,128]{5,4,3,2,1,0:T(8,128)S(1)}) custom-call(f32[24,8,128]{2,1,0:T(8,128)S(1)} %collective-permute-done.halo_ref, f32[2,8,18,2,8,128]{5,4,3,2,1,0:T(8,128)S(1)} %get-tuple-element.71.gauss_in_ref, ...), custom_call_target="tpu_custom_call", output_to_operand_aliasing={{1}: (1, {})} | custom-call | tf_op jit(solution)/shard_map/rest/pallas_call | solution.py:659
  13.2 0.2 %collective-permute-start.2 = (f32[2,32,8,128]{3,2,1,0:T(8,128)S(1)}, f32[2,32,8,128]{3,2,1,0:T(8,128)S(1)}, u32[]{:S(2)}, u32[]{:S(2)}) collective-permute-start(f32[2,32,8,128]{3,2,1,0:T(8,128)S(1)} %get-tuple-element.84.mine_ref), channel_id=1, source_target_pairs={{0,1},{1,0},{2,3},{3,2},{4,5},{5,4},{6,7},{7,6},{8,9},{9,8},{10,11... | collective-permute-start | bytes 786440 | tf_op jit(solution)/shard_map/ppermute | solution.py:665
  13.5 0.8 %put_mine.1.begun_ref = f32[256,512]{1,0:T(8,128)} custom-call(f32[2,32,8,128]{3,2,1,0:T(8,128)S(1)} %get-tuple-element.84.mine_ref), custom_call_target="tpu_custom_call" | custom-call | tf_op jit(solution)/shard_map/put_mine/pallas_call | solution.py:667
  14.3 0.5 %collective-permute-done.2.theirs_ref = f32[2,32,8,128]{3,2,1,0:T(8,128)S(1)} collective-permute-done((f32[2,32,8,128]{3,2,1,0:T(8,128)S(1)}, f32[2,32,8,128]{3,2,1,0:T(8,128)S(1)}, u32[]{:S(2)}, u32[]{:S(2)}) %collective-permute-start.2) | collective-permute-done | bytes 262176 | tf_op jit(solution)/shard_map/ppermute | solution.py:665
  14.8 0.8 %put_theirs.1 = f32[256,512]{1,0:T(8,128)} custom-call(f32[2,32,8,128]{3,2,1,0:T(8,128)S(1)} %collective-permute-done.2.theirs_ref, f32[256,512]{1,0:T(8,128)} %put_mine.1.begun_ref), custom_call_target="tpu_custom_call", output_to_operand_aliasing={{}: (1, {})} | custom-call | tf_op jit(solution)/shard_map/put_theirs/pallas_call | solution.py:668
Async XLA Ops:
  2.3 7.3 %collective-permute-start = (f32[24,8,128]{2,1,0:T(8,128)S(1)}, f32[24,8,128]{2,1,0:T(8,128)S(1)}, u32[]{:S(2)}, u32[]{:S(2)}) collective-permute-start(f32[24,8,128]{2,1,0:T(8,128)S(1)} %get-tuple-element.57), channel_id=1, source_target_pairs={{1,2},{0,15},{3,4},{2,1},{5,6},{4,3},{7,8},{6,5},{9,10},{8,7},{11,... | collective-permute-start | bytes 294920 | tf_op jit(solution)/shard_map/ppermute | solution.py:649
  6.8 1.2 %collective-permute-start.1 = (f32[8,17]{1,0:T(8,128)S(1)}, f32[8,17]{1,0:T(8,128)S(1)}, u32[]{:S(2)}, u32[]{:S(2)}) collective-permute-start(f32[8,17]{1,0:T(8,128)S(1)} %get-tuple-element.58.refs_2_.mine_ref), channel_id=1, source_target_pairs={{0,1},{1,0},{2,3},{3,2},{4,5},{5,4},{6,7},{7,6},{8,9},{9,8},{10,11... | collective-permute-start | bytes 1640 | tf_op jit(solution)/shard_map/ppermute | solution.py:650
  13.2 1.6 %collective-permute-start.2 = (f32[2,32,8,128]{3,2,1,0:T(8,128)S(1)}, f32[2,32,8,128]{3,2,1,0:T(8,128)S(1)}, u32[]{:S(2)}, u32[]{:S(2)}) collective-permute-start(f32[2,32,8,128]{3,2,1,0:T(8,128)S(1)} %get-tuple-element.84.mine_ref), channel_id=1, source_target_pairs={{0,1},{1,0},{2,3},{3,2},{4,5},{5,4},{6,7},{7,6},{8,9},{9,8},{10,11... | collective-permute-start | bytes 786440 | tf_op jit(solution)/shard_map/ppermute | solution.py:665
